TPU v7x, 32 devices: a whole 2x2x4 slice. The times are simulated.
32 devices in a mesh: dp: 8 (over z, x), expert: 4 (over y, core).
Axes of the slice: x: 2, y: 2, z: 4, core: 2. Of those that a mesh axis runs over, the one named last changes fastest.
Arguments:
- tokens: bfloat16 [32, 4096], P(('dp', 'expert')), may hold values from -6 to 6
- cotangent: bfloat16 [32, 4096], P(('dp', 'expert')), may hold values from -1.5 to 1.5
- route_ids: int32 [32, 2], replicated, may hold values from 0 to 3, all different within a row; in each aligned block of 4 rows (0 to 3, 4 to 7, ...) at most 4 rows name the same one
- w_router: bfloat16 [4, 4096], replicated, may hold values from -0.09375 to 0.09375
- w_up: bfloat16 [4, 4096, 8192], P('expert', None, 'dp'), may hold values from -0.09375 to 0.09375
- down_weight: bfloat16 [4, 8192, 4096], P('expert', 'dp'), may hold values from -0.0625 to 0.0625
Outputs:
- grad_up: bfloat16 [4, 4096, 8192], P('expert', None, 'dp')
- grad_down: bfloat16 [4, 8192, 4096], P('expert', 'dp')
- grad_router: float32 [4, 4096], replicated
Inputs may be any that keep to these rules, and one draw needn't show every extreme that they name: `route_ids`: the two ids of a token differ. Within the tokens of one dp index (aligned blocks of 4 rows) no expert is named more than 4 times, a bound that some block reaches.
All inputs are finite; a program needn't handle non-finite values.
Results may differ from a plain program's by a relative error of at most 0.0058.
Values may be sent and summed in bfloat16 or wider, within the bound.
No kernel may reach another device: no remote copies, remote signals or barrier semaphores. Data moves between devices by JAX's collectives and lax.ppermute only.
A program may use at most 128 MiB of HBM per device.

v0:
```python
import jax
import jax.numpy as jnp
from jax import lax
from jax.sharding import PartitionSpec as P


def gate_values(rows_in, pair, w_router):
    logits = lax.dot_general(
        rows_in, w_router, (((1,), (1,)), ((), ())), preferred_element_type=jnp.float32
    )
    columns = jnp.arange(w_router.shape[0], dtype=jnp.int32)
    first_mask = pair[:, 0:1] == columns[None, :]
    second_mask = pair[:, 1:2] == columns[None, :]
    logit_first = jnp.sum(jnp.where(first_mask, logits, 0.0), axis=1)
    logit_second = jnp.sum(jnp.where(second_mask, logits, 0.0), axis=1)
    return (
        first_mask,
        second_mask,
        jax.nn.sigmoid(logit_first - logit_second),
        jax.nn.sigmoid(logit_second - logit_first),
    )


def route_weight(pair, expert_number, p_first, p_second):
    is_first = pair[:, 0] == expert_number
    is_second = pair[:, 1] == expert_number
    return (
        is_first | is_second,
        jnp.where(is_first, p_first, 0.0) + jnp.where(is_second, p_second, 0.0),
    )


def local(tokens, cotangent, route_ids, w_router, w_up, down_weight):
    tok_dev = tokens.shape[0]
    width = tokens.shape[1]
    n_data = lax.axis_size("dp")
    n_experts = lax.axis_size("expert")
    data_index = lax.axis_index("dp")
    expert_index = lax.axis_index("expert")
    block_rows = tok_dev * n_experts
    most_rows = tok_dev * min(6, n_experts)
    own_pair = lax.dynamic_slice_in_dim(
        route_ids, data_index * block_rows + expert_index * tok_dev, tok_dev, 0
    )
    own_first, own_second, own_pfirst, own_psecond = gate_values(tokens, own_pair, w_router)
    block_pair = lax.dynamic_slice_in_dim(route_ids, data_index * block_rows, block_rows, 0)
    block_routed = (block_pair[:, 0] == expert_index) | (block_pair[:, 1] == expert_index)
    block_rank = jnp.cumsum(block_routed.astype(jnp.int32)) - 1
    slot_ids = jnp.arange(most_rows, dtype=jnp.int32)
    select = (block_rank[None, :] == slot_ids[:, None]) & block_routed[None, :]
    x_all, g_all = (
        lax.all_gather(tokens, ("dp", "expert"), axis=0, tiled=True),
        lax.all_gather(cotangent, ("dp", "expert"), axis=0, tiled=True),
    )
    unused_first, unused_second, all_pfirst, all_psecond = gate_values(x_all, route_ids, w_router)
    routed_all, weight_all = route_weight(route_ids, expert_index, all_pfirst, all_psecond)
    g_scaled = (weight_all[:, None] * g_all.astype(jnp.float32)).astype(jnp.bfloat16)
    routed_blocks = routed_all.reshape(n_data, block_rows)
    rank_blocks = jnp.cumsum(routed_blocks.astype(jnp.int32), axis=1) - 1
    pick_all = (
        (rank_blocks[:, None, :] == slot_ids[None, :, None]) & routed_blocks[:, None, :]
    ).astype(jnp.bfloat16)
    x_buf = (
        jnp.einsum(
            "bmt,btd->bmd",
            pick_all,
            x_all.reshape(n_data, block_rows, width),
            preferred_element_type=jnp.float32,
        )
        .astype(jnp.bfloat16)
        .reshape(n_data * most_rows, width)
    )
    g_buf = (
        jnp.einsum(
            "bmt,btd->bmd",
            pick_all,
            g_scaled.reshape(n_data, block_rows, width),
            preferred_element_type=jnp.float32,
        )
        .astype(jnp.bfloat16)
        .reshape(n_data * most_rows, width)
    )
    pre_act = jnp.dot(x_buf, w_up[0], preferred_element_type=jnp.float32)
    returned_gradient = lax.dot_general(
        g_buf, down_weight[0], (((1,), (1,)), ((), ())), preferred_element_type=jnp.float32
    )
    sig_pre = jax.nn.sigmoid(pre_act)
    silu_act = pre_act * sig_pre
    partial_sums = jnp.sum(silu_act * returned_gradient, axis=1)
    hidden_state = silu_act.astype(jnp.bfloat16)
    pre_grad = (returned_gradient * sig_pre * (1.0 + pre_act * (1.0 - sig_pre))).astype(
        jnp.bfloat16
    )
    grad_down = lax.dot_general(
        hidden_state, g_buf, (((0,), (0,)), ((), ())), preferred_element_type=jnp.float32
    ).astype(jnp.bfloat16)
    grad_up = lax.dot_general(
        x_buf, pre_grad, (((0,), (0,)), ((), ())), preferred_element_type=jnp.float32
    ).astype(jnp.bfloat16)
    total_sums = lax.psum(partial_sums, "dp")
    block_sums = lax.dynamic_slice_in_dim(total_sums, data_index * most_rows, most_rows, 0)
    token_sums = jnp.sum(jnp.where(select, block_sums[:, None], 0.0), axis=0)
    came_back = lax.all_to_all(
        token_sums.reshape(n_experts, tok_dev), "expert", split_axis=0, concat_axis=0, tiled=True
    )
    q_first = jnp.sum(jnp.where(own_first.T, came_back, 0.0), axis=0)
    q_second = jnp.sum(jnp.where(own_second.T, came_back, 0.0), axis=0)
    delta = own_psecond * q_first - own_pfirst * q_second
    dlogit = jnp.where(own_first, delta[:, None], 0.0) - jnp.where(own_second, delta[:, None], 0.0)
    router_term = jnp.dot(dlogit.T, tokens.astype(jnp.float32), precision=lax.Precision.HIGHEST)
    grad_router = lax.psum(router_term, ("dp", "expert"))
    return (grad_up[None], grad_down[None], grad_router)


def solution(mesh):
    return jax.shard_map(
        local,
        mesh=mesh,
        in_specs=(
            P(("dp", "expert"), None),
            P(("dp", "expert"), None),
            P(),
            P(),
            P("expert", None, "dp"),
            P("expert", "dp", None),
        ),
        out_specs=(P("expert", None, "dp"), P("expert", "dp", None), P()),
        check_vma=False,
    )
```

profile of v0, /device:TPU:0, one launch (start us, length us, event | category | flops | bytes accessed | tf_op | source)
XLA Modules:
  0.0 271.1 jit_solution(8409192163350090893)
XLA Ops:
  7.2 0.0 copy-start
  7.2 45.0 %all-gather = bf16[32,1,4096]{2,1,0:T(2,128)(2,1)S(1)} all-gather(bf16[1,1,4096]{2,1,0:T(2,128)(2,1)} %bitcast.63), channel_id=1, replica_groups=mesh['dp'=8,'expert'=4] {'dp','expert'}, dimensions={0}, use_global_device_ids=true | all-gather | bytes 270336 | tf_op jit(solution)/shard_map/all_gather | solution.py:52
  52.2 1.5 reduce.7
  53.7 0.1 reshape.260
  53.8 0.8 slice_bitcast_fusion
  54.6 0.8 or_reduce_fusion
  55.4 0.1 or.27
  55.5 0.2 reduce_window_sum.18
  55.6 0.3 convolution_convert_fusion.1
  55.9 0.1 reshape.261
  56.0 38.3 %all-gather.1 = bf16[32,1,4096]{2,1,0:T(2,128)(2,1)S(1)} all-gather(bf16[1,1,4096]{2,1,0:T(2,128)(2,1)} %bitcast.64), channel_id=1, replica_groups=mesh['dp'=8,'expert'=4] {'dp','expert'}, dimensions={0}, use_global_device_ids=true | all-gather | bytes 270336 | tf_op jit(solution)/shard_map/all_gather | solution.py:53
  94.3 0.5 convert_element_type.47
  94.9 0.0 copy-done
  94.9 0.4 select_reduce_fusion.2
  95.3 0.8 fusion.28
  96.1 0.3 fusion.4
  96.4 0.1 reshape.262
  96.5 0.3 convolution_convert_fusion
  96.8 0.1 reshape.263
  96.8 4.9 %fusion = f32[32,1024]{1,0:T(8,128)S(1)} fusion(bf16[32,4096]{1,0:T(8,128)(2,1)S(1)} %reshape.261, bf16[1,4096,1024]{2,1,0:T(8,128)(2,1)} %param.10), kind=kOutput, calls=%fused_computation | convolution fusion | flops 268435456 | bytes 8781824 | tf_op jit(solution)/shard_map/dot_general | solution.py:83
  101.8 0.0 copy-start.2
  101.8 0.0 copy-start.1
  101.8 6.1 %multiply_reduce_fusion = (f32[32]{0:T(128)S(1)}, f32[32,1024]{1,0:T(8,128)S(1)}) fusion(f32[32,1024]{1,0:T(8,128)S(1)} %fusion, bf16[32,4096]{1,0:T(8,128)(2,1)S(1)} %reshape.263, bf16[1,1024,4096]{2,1,0:T(8,128)(2,1)} %param.11), kind=kOutput, calls=%fused_computation.14 | convolution fusion | flops 268632032 | bytes 8913024 | tf_op jit(solution)/shard_map/dot_general | solution.py:84
  107.9 17.1 %psum.14 = f32[32]{0:T(128)S(1)} all-reduce(f32[32]{0:T(128)S(1)} %get-tuple-element.15), channel_id=1, replica_groups=mesh['dp'=8,'expert'=4] {'dp'}, use_global_device_ids=true, to_apply=%region_7.8 | all-reduce | flops 32 | bytes 256 | tf_op jit(solution)/shard_map/psum | solution.py:100
  125.0 0.0 copy-done.2
  125.0 0.1 constant_dynamic-slice_fusion
  125.1 0.1 dynamic_slice.11
  125.2 0.2 reduce-window.8
  125.3 0.1 select_reduce_fusion
  125.4 0.7 copy.11
  126.1 3.5 %all-to-all-start = ((f32[4,1,1]{2,1,0:T(1,128)}), f32[4,1,1]{2,1,0:T(1,128)S(1)}, u32[]{:S(2)}, u32[]{:S(2)}) async-start(f32[4,1,1]{2,1,0:T(1,128)} %copy.11), calls=%async_computation | async-start | bytes 4096 | tf_op jit(solution)/shard_map/all_to_all | solution.py:103
  129.6 0.0 all-reduce.2.cloned.1.call-start
  129.6 0.0 copy-done.1
  129.6 0.1 reduce.9
  129.6 0.1 constant_dynamic-slice_fusion.1
  129.7 0.6 fusion.32
  130.3 2.1 fusion.24
  134.8 5.8 %convert_bitcast_fusion.1 = bf16[1,4096,1024]{2,1,0:T(8,128)(2,1)} fusion(bf16[32,4096]{1,0:T(8,128)(2,1)S(1)} %reshape.261, f32[32,1024]{1,0:T(8,128)S(1)} %fusion, f32[32,1024]{1,0:T(8,128)S(1)} %get-tuple-element.16), kind=kOutput, calls=%fused_computation.5 | convolution fusion | flops 272924672 | bytes 8912896 | tf_op jit(solution)/shard_map/dot_general | solution.py:97
  140.8 0.0 all-to-all-done
  140.8 0.1 reduce.8
  140.9 1.9 fusion.26
  144.0 1.3 fusion.27
  145.4 0.7 broadcast_multiply_fusion
  146.1 0.0 all-reduce.2.cloned.1.call-update
  146.1 5.8 %convert_bitcast_fusion = bf16[1,1024,4096]{2,1,0:T(8,128)(2,1)} fusion(bf16[32,4096]{1,0:T(8,128)(2,1)S(1)} %reshape.263, f32[32,1024]{1,0:T(8,128)S(1)} %fusion), kind=kOutput, calls=%fused_computation.4 | convolution fusion | flops 272793600 | bytes 8781824 | tf_op jit(solution)/shard_map/dot_general | solution.py:94
  151.9 110.8 %all-reduce.2.cloned.1.call-done = f32[4,4096]{1,0:T(4,128)} async-done(((f32[4,4096]{1,0:T(4,128)}), f32[4,4096]{1,0:T(4,128)}) %all-reduce.2.cloned.1.call-update) | async-done | bytes 65552 | tf_op jit(solution)/shard_map/psum | solution.py:111
  262.7 1.5 copy.23
  (5 shorter events, 0.0 us)
Async XLA Ops:
  7.2 87.7 %copy-start = (bf16[4,4096]{1,0:T(4,128)(2,1)S(1)}, bf16[4,4096]{1,0:T(4,128)(2,1)}, u32[]{:S(2)}) copy-start(bf16[4,4096]{1,0:T(4,128)(2,1)} %param.9) | copy-start | bytes 98308
  101.8 23.2 %copy-start.2 = (s32[32,2]{0,1:T(2,128)S(1)}, s32[32,2]{0,1:T(2,128)}, u32[]{:S(2)}) copy-start(s32[32,2]{0,1:T(2,128)} %param.8) | copy-start | bytes 772
  101.8 27.8 %copy-start.1 = (bf16[1,4096]{1,0:T(2,128)(2,1)S(1)}, bf16[1,4096]{1,0:T(2,128)(2,1)}, u32[]{:S(2)}) copy-start(bf16[1,4096]{1,0:T(2,128)(2,1)} %param.6) | copy-start | bytes 24580
  126.1 14.7 %all-to-all-start = ((f32[4,1,1]{2,1,0:T(1,128)}), f32[4,1,1]{2,1,0:T(1,128)S(1)}, u32[]{:S(2)}, u32[]{:S(2)}) async-start(f32[4,1,1]{2,1,0:T(1,128)} %copy.11), calls=%async_computation | async-start | bytes 4096 | tf_op jit(solution)/shard_map/all_to_all | solution.py:103
  129.6 133.2 %all-reduce.2.cloned.1.call-start = ((), (), s32[]{:S(2)}) async-start(), calls=%async_computation.1 | async-start | bytes 131072 | tf_op jit(solution)/shard_map/psum | solution.py:111
Sparse Core Ops, SparseCore 0:
  146.2 116.4 all-reduce.1
where the time goes:
time: 273 us; the launch traced here: 271 us
  waiting for transfers between devices  111 us (41%)
  blocking collectives  100 us (37%)
  matrix products  25.7 us (9%)
  between operations  18 us (7%)
  other arithmetic  8.52 us (3%)
  local copies, waits for them, and re-layouts  4.16 us (2%)
  starting transfers between devices  3.46 us (1%)
    psum x1, waiting for transfers between devices, local(): grad_router = lax.psum(router_term, ('dp', 'expert'))  111 us
    all_gather x1, blocking collectives, local(): lax.all_gather(tokens, ('dp', 'expert'), axis=0, tiled=True)  45 us
    all_gather x1, blocking collectives, local(): lax.all_gather(cotangent, ('dp', 'expert'), axis=0, tiled=True)  38.3 us
    psum x1, blocking collectives, local(): total_sums = lax.psum(partial_sums, 'dp')  17.1 us
    dot_general x1, matrix products, local(): lax.dot_general(g_buf, down_weight[0], (((1,), (1,)), ((), ())), preferre...  6.09 us
    dot_general x1, matrix products, local(): lax.dot_general(hidden_state, g_buf, (((0,), (0,)), ((), ())), preferred_...  5.79 us
    dot_general x1, matrix products, local(): lax.dot_general(x_buf, pre_grad, (((0,), (0,)), ((), ())), preferred_elem...  5.78 us
  transfers between devices with their start and end apart: 2, of which 1 were waited for; matrix products, arithmetic and copies ran while one was open for 5% of the time, Pallas kernels for 0%

commit v1 on v0

v1 whole, which is shorter than its diff:
```python
import functools

import jax
import jax.numpy as jnp
from jax import lax
from jax.experimental import pallas as pl
from jax.experimental.pallas import tpu as pltpu
from jax.sharding import PartitionSpec as P

F32 = jnp.float32
BF16 = jnp.bfloat16
AXES = ("dp", "expert")
VMEM_LIMIT = 56 * 1024 * 1024


def gather_rows(row, n):
    order = [0]
    bit = n // 2
    while bit:
        other = lax.ppermute(row, AXES, [(i, i ^ bit) for i in range(n)])
        row = jnp.concatenate([row, other], axis=0)
        order = order + [o ^ bit for o in order]
        bit //= 2
    return row, order


def one_hot(row_tok, rows):
    return row_tok == lax.broadcasted_iota(jnp.int32, (rows, rows), 1)


def forward_kernel(
    who, row_tok, ids, w_router, xg, w_up, down, hidden, dpre, gs, terms, up_buf, down_buf, sems
):
    rows = xg.shape[0]
    width = w_up.shape[0]
    ff = w_up.shape[1]
    chunks = sems.shape[1]
    kc = width // chunks
    fc = ff // chunks
    ups = [
        pltpu.make_async_copy(w_up.at[pl.ds(i * kc, kc)], up_buf.at[pl.ds(i * kc, kc)], sems.at[0, i])
        for i in range(chunks)
    ]
    downs = [
        pltpu.make_async_copy(down.at[pl.ds(i * fc, fc)], down_buf.at[pl.ds(i * fc, fc)], sems.at[1, i])
        for i in range(chunks)
    ]
    for c in ups + downs:
        c.start()
    expert = who[0, 0]
    perm = one_hot(row_tok[...], rows)
    pair = jnp.dot(
        perm.astype(BF16), ids[...].astype(F32).astype(BF16), preferred_element_type=F32
    ).astype(jnp.int32)
    logits = lax.dot_general(
        xg[:, :width], w_router[...], (((1,), (1,)), ((), ())), preferred_element_type=F32
    )
    columns = lax.broadcasted_iota(jnp.int32, logits.shape, 1)
    first = pair[:, 0:1]
    second = pair[:, 1:2]
    l0 = jnp.sum(jnp.where(first == columns, logits, 0.0), axis=1, keepdims=True)
    l1 = jnp.sum(jnp.where(second == columns, logits, 0.0), axis=1, keepdims=True)
    p0 = jax.nn.sigmoid(l0 - l1)
    p1 = jax.nn.sigmoid(l1 - l0)
    is0 = first == expert
    is1 = second == expert
    weight = jnp.where(is0, p0, 0.0) + jnp.where(is1, p1, 0.0)
    gs[...] = (weight * xg[:, width:].astype(F32)).astype(BF16)
    pre = jnp.zeros((rows, ff), F32)
    for i in range(chunks):
        ups[i].wait()
        pre = pre + jnp.dot(
            xg[:, i * kc : (i + 1) * kc], up_buf[i * kc : (i + 1) * kc, :], preferred_element_type=F32
        )
    sig = jax.nn.sigmoid(pre)
    silu = pre * sig
    slope = sig * (1.0 + pre * (1.0 - sig))
    hidden[...] = silu.astype(BF16)
    q = jnp.zeros((rows, 1), F32)
    for i in range(chunks):
        downs[i].wait()
        back = lax.dot_general(
            gs[...],
            down_buf[i * fc : (i + 1) * fc, :],
            (((1,), (1,)), ((), ())),
            preferred_element_type=F32,
        )
        part = slice(i * fc, (i + 1) * fc)
        q = q + jnp.sum(silu[:, part] * back, axis=1, keepdims=True)
        dpre[:, part] = (back * slope[:, part]).astype(BF16)
    dl = (jnp.where(is0, p1, 0.0) - jnp.where(is1, p0, 0.0)) * q
    line = jnp.sum(jnp.where(perm, dl, 0.0), axis=0, keepdims=True)
    terms[...] = jnp.broadcast_to(line[None], terms.shape)


def forward(who, row_tok, ids, w_router, xg, w_up, down, n):
    rows = xg.shape[0]
    width, ff = w_up.shape
    chunks = 8 if ff % 1024 == 0 else 1
    vm = pl.BlockSpec(memory_space=pltpu.VMEM)
    hbm = pl.BlockSpec(memory_space=pltpu.HBM)
    return pl.pallas_call(
        forward_kernel,
        out_shape=(
            jax.ShapeDtypeStruct((rows, ff), BF16),
            jax.ShapeDtypeStruct((rows, ff), BF16),
            jax.ShapeDtypeStruct((rows, width), BF16),
            jax.ShapeDtypeStruct((n, 1, rows), F32),
        ),
        in_specs=[pl.BlockSpec(memory_space=pltpu.SMEM), vm, vm, vm, vm, hbm, hbm],
        out_specs=(vm, vm, vm, vm),
        scratch_shapes=[
            pltpu.VMEM(w_up.shape, BF16),
            pltpu.VMEM(down.shape, BF16),
            pltpu.SemaphoreType.DMA((2, chunks)),
        ],
        compiler_params=pltpu.CompilerParams(vmem_limit_bytes=VMEM_LIMIT),
        name="forward",
    )(who, row_tok, ids, w_router, xg, w_up, down)


def grads_kernel(x, hidden, dpre, gs, up_out, down_out):
    up_out[...] = lax.dot_general(
        x[...], dpre[...], (((0,), (0,)), ((), ())), preferred_element_type=F32
    ).astype(BF16)
    down_out[...] = lax.dot_general(
        hidden[...], gs[...], (((0,), (0,)), ((), ())), preferred_element_type=F32
    ).astype(BF16)


def grads(xg, hidden, dpre, gs):
    rows, ff = hidden.shape
    width = gs.shape[1]
    steps = 8 if ff % 1024 == 0 else 1
    kc, fc = width // steps, ff // steps
    return pl.pallas_call(
        grads_kernel,
        grid=(steps,),
        out_shape=(
            jax.ShapeDtypeStruct((width, ff), BF16),
            jax.ShapeDtypeStruct((ff, width), BF16),
        ),
        in_specs=[
            pl.BlockSpec((rows, kc), lambda i: (0, i)),
            pl.BlockSpec((rows, fc), lambda i: (0, i)),
            pl.BlockSpec((rows, ff), lambda i: (0, 0)),
            pl.BlockSpec((rows, width), lambda i: (0, 0)),
        ],
        out_specs=(
            pl.BlockSpec((kc, ff), lambda i: (i, 0)),
            pl.BlockSpec((fc, width), lambda i: (i, 0)),
        ),
        compiler_params=pltpu.CompilerParams(vmem_limit_bytes=VMEM_LIMIT),
        name="grads",
    )(xg, hidden, dpre, gs)


def router_kernel(terms, row_tok, ids, xg, out):
    rows = xg.shape[0]
    width = out.shape[1]
    dl = jnp.sum(terms[...], axis=0)
    perm = one_hot(row_tok[...], rows).astype(BF16)
    x = lax.dot_general(
        perm, xg[:, :width], (((0,), (0,)), ((), ())), preferred_element_type=F32
    ).astype(BF16)
    experts = lax.broadcasted_iota(jnp.int32, (out.shape[0], rows), 0)
    dlogit = jnp.where(ids[0:1, :] == experts, dl, 0.0) - jnp.where(ids[1:2, :] == experts, dl, 0.0)
    high = dlogit.astype(BF16)
    rest = dlogit - high.astype(F32)
    mid = rest.astype(BF16)
    low = (rest - mid.astype(F32)).astype(BF16)
    dot = functools.partial(jnp.dot, preferred_element_type=F32)
    out[...] = dot(low, x) + dot(mid, x) + dot(high, x)


def router(terms, row_tok, ids_t, xg, n_experts, width):
    vm = pl.BlockSpec(memory_space=pltpu.VMEM)
    return pl.pallas_call(
        router_kernel,
        out_shape=jax.ShapeDtypeStruct((n_experts, width), F32),
        in_specs=[vm] * 4,
        out_specs=vm,
        compiler_params=pltpu.CompilerParams(vmem_limit_bytes=VMEM_LIMIT),
        name="router",
    )(terms, row_tok, ids_t, xg)


def local(tokens, cotangent, route_ids, w_router, w_up, down_weight):
    n = lax.axis_size("dp") * lax.axis_size("expert")
    me = lax.axis_index("dp") * lax.axis_size("expert") + lax.axis_index("expert")
    who = lax.axis_index("expert").astype(jnp.int32).reshape(1, 1)
    xg, order = gather_rows(jnp.concatenate([tokens, cotangent], axis=1), n)
    row_tok = (jnp.asarray(order, jnp.int32) ^ me).reshape(n, 1)
    hidden, dpre, gs, terms = forward(
        who, row_tok, route_ids, w_router, xg, w_up[0], down_weight[0], n
    )
    terms = lax.all_to_all(terms, AXES, 0, 0, tiled=True)
    grad_up, grad_down = grads(xg, hidden, dpre, gs)
    grad_router = router(terms, row_tok, route_ids.T, xg, w_router.shape[0], tokens.shape[1])
    return (grad_up[None], grad_down[None], grad_router)


def solution(mesh):
    return jax.shard_map(
        local,
        mesh=mesh,
        in_specs=(
            P(AXES, None),
            P(AXES, None),
            P(),
            P(),
            P("expert", None, "dp"),
            P("expert", "dp", None),
        ),
        out_specs=(P("expert", None, "dp"), P("expert", "dp", None), P()),
        check_vma=False,
    )
```

time: 273 us -> 57.4 us (0.21)
  waiting for transfers between devices: 111 us -> 10.4 us
  blocking collectives: 100 us -> 0 us
  matrix products: 25.7 us -> 0 us
  Pallas kernels: 0 us -> 22.6 us
  between operations: 18 us -> 0.69 us
  starting transfers between devices: 3.46 us -> 15.5 us
  other arithmetic: 8.52 us -> 1.01 us
    psum x1 -> x0, waiting for transfers between devices: 111 us -> none  [local(): grad_router = lax.psum(router_term, ('dp', 'expert'))]
    all_gather x2 -> x0, blocking collectives: 83.3 us -> none  [the longest x1 45 us: local(): lax.all_gather(tokens, ('dp', 'expert'), axis=0, tiled=True)]
    dot_general x8 -> x0, matrix products: 25.7 us -> none  [the longest x1 6.09 us: local(): lax.dot_general(g_buf, down_weight[0], (((1,), (1,)), ((), ())), preferre...]
    pallas_call x0 -> x3, Pallas kernels: none -> 22.6 us  [the longest x1 11.6 us: forward(): pl.pallas_call(forward_kernel, out_shape=(jax.ShapeDtypeStruct((rows, ff)...]
    psum x1 -> x0, blocking collectives: 17.1 us -> none  [local(): total_sums = lax.psum(partial_sums, 'dp')]
    ppermute x0 -> x5, waiting for transfers between devices: none -> 10.4 us  [gather_rows(): other = lax.ppermute(row, AXES, [(i, i ^ bit) for i in range(n)])]
    ppermute x0 -> x5, starting transfers between devices: none -> 9.35 us  [gather_rows(): other = lax.ppermute(row, AXES, [(i, i ^ bit) for i in range(n)])]
    concatenate x0 -> x3, local copies, waits for them, and re-layouts: none -> 3.16 us  [the longest x2 2.42 us: gather_rows(): row = jnp.concatenate([row, other], axis=0)]
  transfers between devices with their start and end apart: 2 -> 6, of which waited for: 1 -> 4; matrix products, arithmetic and copies ran while one was open for 5% -> 5% of each run, Pallas kernels for 0% -> 15%
where the time goes in v1:
time: 57.4 us; the launch traced here: 56.8 us
  Pallas kernels  22.6 us (39%)
  starting transfers between devices  15.5 us (27%)
  waiting for transfers between devices  10.4 us (18%)
  local copies, waits for them, and re-layouts  6.55 us (11%)
  other arithmetic  1.01 us (2%)
  between operations  0.69 us (1%)
    pallas_call x1, Pallas kernels, forward(): pl.pallas_call(forward_kernel, out_shape=(jax.ShapeDtypeStruct((rows, ff)...  11.6 us
    ppermute x5, waiting for transfers between devices, gather_rows(): other = lax.ppermute(row, AXES, [(i, i ^ bit) for i in range(n)])  10.4 us
    ppermute x5, starting transfers between devices, gather_rows(): other = lax.ppermute(row, AXES, [(i, i ^ bit) for i in range(n)])  9.35 us
    pallas_call x1, Pallas kernels, grads(): pl.pallas_call(grads_kernel, grid=(steps,), out_shape=(jax.ShapeDtypeStru...  8.79 us
    all_to_all x1, starting transfers between devices, local(): terms = lax.all_to_all(terms, AXES, 0, 0, tiled=True)  6.16 us
    unnamed x4, local copies, waits for them, and re-layouts  2.69 us
    concatenate x2, local copies, waits for them, and re-layouts, gather_rows(): row = jnp.concatenate([row, other], axis=0)  2.42 us
    pallas_call x1, Pallas kernels, router(): pl.pallas_call(router_kernel, out_shape=jax.ShapeDtypeStruct((n_experts,...  2.25 us
  transfers between devices with their start and end apart: 6, of which 4 were waited for; matrix products, arithmetic and copies ran while one was open for 5% of the time, Pallas kernels for 15%

profile of v1, /device:TPU:0, one launch (start us, length us, event | category | flops | bytes accessed | tf_op | source)
XLA Modules:
  0.0 56.8 jit_solution(6100527883000772611)
XLA Ops:
  0.6 0.7 %constant_dynamic-update-slice_fusion.1 = bf16[1,8192]{1,0:T(2,128)(2,1)S(1)} fusion(bf16[1,4096]{1,0:T(2,128)(2,1)} %param.7), kind=kLoop, calls=%fused_computation.4 | loop fusion | bytes 24576
  1.4 0.7 %constant_dynamic-update-slice_fusion = bf16[1,8192]{1,0:T(2,128)(2,1)S(1)} fusion(bf16[1,8192]{1,0:T(2,128)(2,1)S(1)} %constant_dynamic-update-slice_fusion.1, bf16[1,4096]{1,0:T(2,128)(2,1)} %param.8), kind=kLoop, calls=%fused_computation.3 | loop fusion | bytes 24576 | tf_op jit(solution)/shard_map/concatenate | solution.py:192
  2.1 4.1 %collective-permute-start = (bf16[1,8192]{1,0:T(2,128)(2,1)S(1)}, bf16[1,8192]{1,0:T(2,128)(2,1)S(1)}, u32[]{:S(2)}, u32[]{:S(2)}) collective-permute-start(bf16[1,8192]{1,0:T(2,128)(2,1)S(1)} %constant_dynamic-update-slice_fusion), channel_id=1, source_target_pairs={{0,16},{1,17},{2,18},{3,19},{4,20},{5,21},{6,22},{7,23},{8,24},{9,... | collective-permute-start | bytes 49160 | tf_op jit(solution)/shard_map/ppermute | solution.py:20
  6.2 2.2 %collective-permute-done = bf16[1,8192]{1,0:T(2,128)(2,1)S(1)} collective-permute-done((bf16[1,8192]{1,0:T(2,128)(2,1)S(1)}, bf16[1,8192]{1,0:T(2,128)(2,1)S(1)}, u32[]{:S(2)}, u32[]{:S(2)}) %collective-permute-start) | collective-permute-done | bytes 16416 | tf_op jit(solution)/shard_map/ppermute | solution.py:20
  8.5 0.1 pad_maximum_fusion.2
  8.5 1.6 %collective-permute-start.1 = (bf16[2,8192]{1,0:T(2,128)(2,1)S(1)}, bf16[2,8192]{1,0:T(2,128)(2,1)S(1)}, u32[]{:S(2)}, u32[]{:S(2)}) collective-permute-start(bf16[2,8192]{1,0:T(2,128)(2,1)S(1)} %pad_maximum_fusion.2), channel_id=1, source_target_pairs={{0,8},{1,9},{2,10},{3,11},{4,12},{5,13},{6,14},{7,15},{8,0},{9,1},... | collective-permute-start | bytes 98312 | tf_op jit(solution)/shard_map/ppermute | solution.py:20
  10.2 2.4 %collective-permute-done.1 = bf16[2,8192]{1,0:T(2,128)(2,1)S(1)} collective-permute-done((bf16[2,8192]{1,0:T(2,128)(2,1)S(1)}, bf16[2,8192]{1,0:T(2,128)(2,1)S(1)}, u32[]{:S(2)}, u32[]{:S(2)}) %collective-permute-start.1) | collective-permute-done | bytes 32800 | tf_op jit(solution)/shard_map/ppermute | solution.py:20
  12.5 0.1 pad_maximum_fusion.1
  12.6 1.8 %collective-permute-start.2 = (bf16[4,8192]{1,0:T(4,128)(2,1)S(1)}, bf16[4,8192]{1,0:T(4,128)(2,1)S(1)}, u32[]{:S(2)}, u32[]{:S(2)}) collective-permute-start(bf16[4,8192]{1,0:T(4,128)(2,1)S(1)} %pad_maximum_fusion.1), channel_id=1, source_target_pairs={{0,4},{1,5},{2,6},{3,7},{4,0},{5,1},{6,2},{7,3},{8,12},{9,13},{10,... | collective-permute-start | bytes 196616 | tf_op jit(solution)/shard_map/ppermute | solution.py:20
  14.4 2.6 %collective-permute-done.2 = bf16[4,8192]{1,0:T(4,128)(2,1)S(1)} collective-permute-done((bf16[4,8192]{1,0:T(4,128)(2,1)S(1)}, bf16[4,8192]{1,0:T(4,128)(2,1)S(1)}, u32[]{:S(2)}, u32[]{:S(2)}) %collective-permute-start.2) | collective-permute-done | bytes 65568 | tf_op jit(solution)/shard_map/ppermute | solution.py:20
  17.0 0.2 pad_maximum_fusion
  17.1 1.8 %collective-permute-start.3 = (bf16[8,8192]{1,0:T(8,128)(2,1)S(1)}, bf16[8,8192]{1,0:T(8,128)(2,1)S(1)}, u32[]{:S(2)}, u32[]{:S(2)}) collective-permute-start(bf16[8,8192]{1,0:T(8,128)(2,1)S(1)} %pad_maximum_fusion), channel_id=1, source_target_pairs={{0,2},{1,3},{2,0},{3,1},{4,6},{5,7},{6,4},{7,5},{8,10},{9,11},{10,... | collective-permute-start | bytes 393224 | tf_op jit(solution)/shard_map/ppermute | solution.py:20
  18.9 3.2 %collective-permute-done.3 = bf16[8,8192]{1,0:T(8,128)(2,1)S(1)} collective-permute-done((bf16[8,8192]{1,0:T(8,128)(2,1)S(1)}, bf16[8,8192]{1,0:T(8,128)(2,1)S(1)}, u32[]{:S(2)}, u32[]{:S(2)}) %collective-permute-start.3) | collective-permute-done | bytes 131104 | tf_op jit(solution)/shard_map/ppermute | solution.py:20
  22.2 0.2 concatenate.26
  22.4 0.1 collective-permute-start.4
  22.4 0.7 %xor_bitcast_fusion = s32[32,1]{0,1:T(1,128)S(1)} fusion(s32[32]{0:T(128)} %constant.13.clone, s32[]{:T(128)S(6)} %add.3), kind=kLoop, calls=%fused_computation.5 | loop fusion | flops 32 | bytes 260 | tf_op jit(solution)/shard_map/reshape | solution.py:193
  23.1 0.7 %copy.10.row_tok = s32[32,1]{1,0:T(8,128)} copy(s32[32,1]{0,1:T(1,128)S(1)} %xor_bitcast_fusion) | data formatting | bytes 256 | tf_op jit(solution)/shard_map/reshape | solution.py:193
  23.8 1.4 %copy.11.ids = s32[32,2]{1,0:T(8,128)} copy(s32[32,2]{0,1:T(2,128)} %param.9) | data formatting | bytes 512 | tf_op args[2]
  25.2 0.0 collective-permute-done.4
  25.2 2.2 %concatenate.27.xg.x = bf16[32,8192]{1,0:T(8,128)(2,1)} concatenate(bf16[1,8192]{1,0:T(2,128)(2,1)S(1)} %constant_dynamic-update-slice_fusion, bf16[1,8192]{1,0:T(2,128)(2,1)S(1)} %collective-permute-done, bf16[2,8192]{1,0:T(2,128)(2,1)S(1)} %collective-permute-done.1, bf16[4,8192]{1,0:T(4,128)(2,1)S(1)} %collective-permute-done.2, bf16[8,8192]{1,0:T(8,128)(2,1)S(1)} %collective-permute-done.3, ...), dimensions={0} | concatenate | bytes 1048576 | tf_op jit(solution)/shard_map/concatenate | solution.py:21
  27.4 11.6 %forward.1 = (bf16[32,1024]{1,0:T(8,128)(2,1)}, bf16[32,1024]{1,0:T(8,128)(2,1)}, bf16[32,4096]{1,0:T(8,128)(2,1)}, f32[32,1,32]{2,1,0:T(1,128)}) custom-call(s32[1,1]{1,0:T(1,128)} %bitcast.who, s32[32,1]{1,0:T(8,128)} %copy.10.row_tok, s32[32,2]{1,0:T(8,128)} %copy.11.ids, bf16[4,4096]{1,0:T(4,128)(2,1)} %w_router.1, bf16[32,8192]{1,0:T(8,128)(2,1)} %concatenate.27.xg.x, ...), custom_call_target="tpu_custom_call" | custom-call | tf_op jit(solution)/shard_map/forward/pallas_call | solution.py:102
  39.0 6.2 %all-to-all-start = ((f32[32,1,32]{2,1,0:T(1,128)}), f32[32,1,32]{2,1,0:T(1,128)S(1)}, u32[]{:S(2)}, u32[]{:S(2)}) async-start(f32[32,1,32]{2,1,0:T(1,128)} %get-tuple-element.14), calls=%async_computation | async-start | bytes 32768 | tf_op jit(solution)/shard_map/all_to_all | solution.py:197
  45.1 8.8 %grads.1 = (bf16[4096,1024]{1,0:T(8,128)(2,1)}, bf16[1024,4096]{1,0:T(8,128)(2,1)}) custom-call(bf16[32,8192]{1,0:T(8,128)(2,1)} %concatenate.27.xg.x, bf16[32,1024]{1,0:T(8,128)(2,1)} %get-tuple-element.9.hidden, bf16[32,1024]{1,0:T(8,128)(2,1)} %get-tuple-element.10.dpre, bf16[32,4096]{1,0:T(8,128)(2,1)} %get-tuple-element.11.gs), custom_call_target="tpu_custom_call" | custom-call | tf_op jit(solution)/shard_map/grads/pallas_call | solution.py:136
  53.9 0.0 all-to-all-done.terms
  53.9 0.0 copy-start
  53.9 0.6 %copy-done = f32[32,1,32]{2,1,0:T(1,128)} copy-done((f32[32,1,32]{2,1,0:T(1,128)}, f32[32,1,32]{2,1,0:T(1,128)S(1)}, u32[]{:S(2)}) %copy-start) | copy-done | bytes 4120
  54.5 2.3 %router.1 = f32[4,4096]{1,0:T(4,128)} custom-call(f32[32,1,32]{2,1,0:T(1,128)} %copy-done, s32[32,1]{1,0:T(8,128)} %copy.10.row_tok, s32[2,32]{1,0:T(2,128)} %bitcast.10, bf16[32,8192]{1,0:T(8,128)(2,1)} %concatenate.27.xg.x), custom_call_target="tpu_custom_call" | custom-call | tf_op jit(solution)/shard_map/router/pallas_call | solution.py:178
Async XLA Ops:
  2.1 6.3 %collective-permute-start = (bf16[1,8192]{1,0:T(2,128)(2,1)S(1)}, bf16[1,8192]{1,0:T(2,128)(2,1)S(1)}, u32[]{:S(2)}, u32[]{:S(2)}) collective-permute-start(bf16[1,8192]{1,0:T(2,128)(2,1)S(1)} %constant_dynamic-update-slice_fusion), channel_id=1, source_target_pairs={{0,16},{1,17},{2,18},{3,19},{4,20},{5,21},{6,22},{7,23},{8,24},{9,... | collective-permute-start | bytes 49160 | tf_op jit(solution)/shard_map/ppermute | solution.py:20
  8.5 4.0 %collective-permute-start.1 = (bf16[2,8192]{1,0:T(2,128)(2,1)S(1)}, bf16[2,8192]{1,0:T(2,128)(2,1)S(1)}, u32[]{:S(2)}, u32[]{:S(2)}) collective-permute-start(bf16[2,8192]{1,0:T(2,128)(2,1)S(1)} %pad_maximum_fusion.2), channel_id=1, source_target_pairs={{0,8},{1,9},{2,10},{3,11},{4,12},{5,13},{6,14},{7,15},{8,0},{9,1},... | collective-permute-start | bytes 98312 | tf_op jit(solution)/shard_map/ppermute | solution.py:20
  12.6 4.3 %collective-permute-start.2 = (bf16[4,8192]{1,0:T(4,128)(2,1)S(1)}, bf16[4,8192]{1,0:T(4,128)(2,1)S(1)}, u32[]{:S(2)}, u32[]{:S(2)}) collective-permute-start(bf16[4,8192]{1,0:T(4,128)(2,1)S(1)} %pad_maximum_fusion.1), channel_id=1, source_target_pairs={{0,4},{1,5},{2,6},{3,7},{4,0},{5,1},{6,2},{7,3},{8,12},{9,13},{10,... | collective-permute-start | bytes 196616 | tf_op jit(solution)/shard_map/ppermute | solution.py:20
  17.1 5.0 %collective-permute-start.3 = (bf16[8,8192]{1,0:T(8,128)(2,1)S(1)}, bf16[8,8192]{1,0:T(8,128)(2,1)S(1)}, u32[]{:S(2)}, u32[]{:S(2)}) collective-permute-start(bf16[8,8192]{1,0:T(8,128)(2,1)S(1)} %pad_maximum_fusion), channel_id=1, source_target_pairs={{0,2},{1,3},{2,0},{3,1},{4,6},{5,7},{6,4},{7,5},{8,10},{9,11},{10,... | collective-permute-start | bytes 393224 | tf_op jit(solution)/shard_map/ppermute | solution.py:20
  22.4 2.8 %collective-permute-start.4 = (bf16[16,8192]{1,0:T(8,128)(2,1)S(1)}, bf16[16,8192]{1,0:T(8,128)(2,1)S(1)}, u32[]{:S(2)}, u32[]{:S(2)}) collective-permute-start(bf16[16,8192]{1,0:T(8,128)(2,1)S(1)} %concatenate.26), channel_id=1, source_target_pairs={{0,1},{1,0},{2,3},{3,2},{4,5},{5,4},{6,7},{7,6},{8,9},{9,8},{10,11... | collective-permute-start | bytes 786440 | tf_op jit(solution)/shard_map/ppermute | solution.py:20
  39.0 15.0 %all-to-all-start = ((f32[32,1,32]{2,1,0:T(1,128)}), f32[32,1,32]{2,1,0:T(1,128)S(1)}, u32[]{:S(2)}, u32[]{:S(2)}) async-start(f32[32,1,32]{2,1,0:T(1,128)} %get-tuple-element.14), calls=%async_computation | async-start | bytes 32768 | tf_op jit(solution)/shard_map/all_to_all | solution.py:197
  53.9 0.6 %copy-start = (f32[32,1,32]{2,1,0:T(1,128)}, f32[32,1,32]{2,1,0:T(1,128)S(1)}, u32[]{:S(2)}) copy-start(f32[32,1,32]{2,1,0:T(1,128)S(1)} %all-to-all-done.terms) | copy-start | bytes 12292

commit v2 on v1

v2 whole, which is shorter than its diff:
```python
import functools

import jax
import jax.numpy as jnp
from jax import lax
from jax.experimental import pallas as pl
from jax.experimental.pallas import tpu as pltpu
from jax.sharding import Mesh, PartitionSpec as P

F32 = jnp.float32
BF16 = jnp.bfloat16
CHIPS = ("dp", "ey")
AXES = ("dp", "ey", "core")
MIB = 1024 * 1024
VM = pl.BlockSpec(memory_space=pltpu.VMEM)
HBM = pl.BlockSpec(memory_space=pltpu.HBM)


def dot(a, b, ca=1, cb=0):
    return lax.dot_general(a, b, (((ca,), (cb,)), ((), ())), preferred_element_type=F32)


def in_hbm(x):
    return pltpu.with_memory_space_constraint(x, pltpu.HBM)


def pack_kernel(tokens, cotangent, out, buf, sems):
    loads = [
        pltpu.make_async_copy(ref, buf.at[i], sems.at[i]) for i, ref in enumerate((tokens, cotangent))
    ]
    for c in loads:
        c.start()
    for c in loads:
        c.wait()
    both = jnp.concatenate([buf[0], buf[1]], axis=0)
    out[...] = jnp.broadcast_to(both[None], out.shape)


def pack(tokens, cotangent, n):
    return pl.pallas_call(
        pack_kernel,
        out_shape=pltpu.VMEM((n, 2, tokens.shape[1]), BF16),
        in_specs=[HBM, HBM],
        out_specs=VM,
        scratch_shapes=[pltpu.VMEM((2,) + tokens.shape, BF16), pltpu.SemaphoreType.DMA((2,))],
        compiler_params=pltpu.CompilerParams(vmem_limit_bytes=16 * MIB),
        name="pack",
    )(in_hbm(tokens), in_hbm(cotangent))


def token_of_row(rows, core, shape, dim):
    row = lax.broadcasted_iota(jnp.int32, shape, dim)
    half = rows // 2
    return jnp.where(row < half, 2 * row + core, 2 * (row - half) + 1 - core)


def forward_kernel(
    chunks,
    ids_in,
    gate_in,
    mine,
    other,
    w_up,
    down,
    x,
    gs,
    hidden,
    dpre,
    terms,
    ids,
    gate,
    up_buf,
    down_buf,
    sems,
):
    rows, width = x.shape
    kc = width // chunks
    half = rows // 2
    small = [
        pltpu.make_async_copy(gate_in, gate, sems.at[2, 0]),
        pltpu.make_async_copy(ids_in, ids, sems.at[2, 1]),
    ]
    ups, downs = [], []
    for i in range(chunks):
        part = pl.ds(i * kc, kc)
        downs.append(pltpu.make_async_copy(down.at[:, part], down_buf.at[:, part], sems.at[0, i]))
        ups.append(pltpu.make_async_copy(w_up.at[part], up_buf.at[part], sems.at[1, i]))
    for c in small + downs + ups:
        c.start()
    expert = 2 * lax.axis_index("ey") + lax.axis_index("core")
    core = lax.axis_index("core")
    x[:half, :] = mine[:, 0, :]
    x[half:, :] = other[:, 0, :]
    for c in small:
        c.wait()
    place = lax.broadcasted_iota(jnp.int32, (rows, rows), 1)
    perm = token_of_row(rows, core, (rows, rows), 0) == place
    first = jnp.sum(jnp.where(perm, ids[0:1, :], 0), axis=1, keepdims=True)
    second = jnp.sum(jnp.where(perm, ids[1:2, :], 0), axis=1, keepdims=True)
    logits = dot(x[...], gate[...], 1, 1)
    columns = lax.broadcasted_iota(jnp.int32, logits.shape, 1)
    l0 = jnp.sum(jnp.where(first == columns, logits, 0.0), axis=1, keepdims=True)
    l1 = jnp.sum(jnp.where(second == columns, logits, 0.0), axis=1, keepdims=True)
    p0 = jax.nn.sigmoid(l0 - l1)
    p1 = jax.nn.sigmoid(l1 - l0)
    is0 = first == expert
    is1 = second == expert
    weight = jnp.where(is0, p0, 0.0) + jnp.where(is1, p1, 0.0)
    gs[:half, :] = (weight[:half] * mine[:, 1, :].astype(F32)).astype(BF16)
    gs[half:, :] = (weight[half:] * other[:, 1, :].astype(F32)).astype(BF16)
    back = None
    for i in range(chunks):
        downs[i].wait()
        part = slice(i * kc, (i + 1) * kc)
        term = dot(gs[:, part], down_buf[:, part], 1, 1)
        back = term if back is None else back + term
    pre = None
    for i in range(chunks):
        ups[i].wait()
        part = slice(i * kc, (i + 1) * kc)
        term = dot(x[:, part], up_buf[part, :])
        pre = term if pre is None else pre + term
    sig = jax.nn.sigmoid(pre)
    silu = pre * sig
    hidden[...] = silu.astype(BF16)
    dpre[...] = (back * sig * (1.0 + pre * (1.0 - sig))).astype(BF16)
    q = jnp.sum(silu * back, axis=1, keepdims=True)
    dl = (jnp.where(is0, p1, 0.0) - jnp.where(is1, p0, 0.0)) * q
    line = jnp.sum(jnp.where(perm, dl, 0.0), axis=0, keepdims=True)
    terms[...] = jnp.broadcast_to(line[None], terms.shape)


def forward(ids, w_router, mine, other, w_up, down):
    rows = 2 * mine.shape[0]
    width, ff = w_up.shape
    chunks = 8
    return pl.pallas_call(
        functools.partial(forward_kernel, chunks),
        out_shape=(
            pltpu.VMEM((rows, width), BF16),
            pltpu.VMEM((rows, width), BF16),
            pltpu.VMEM((rows, ff), BF16),
            pltpu.VMEM((rows, ff), BF16),
            pltpu.VMEM((rows, 1, rows), F32),
        ),
        in_specs=[HBM] * 2 + [VM] * 2 + [HBM] * 2,
        out_specs=(VM,) * 5,
        scratch_shapes=[
            pltpu.VMEM(ids.shape, jnp.int32),
            pltpu.VMEM(w_router.shape, BF16),
            pltpu.VMEM(w_up.shape, BF16),
            pltpu.VMEM(down.shape, BF16),
            pltpu.SemaphoreType.DMA((3, chunks)),
        ],
        compiler_params=pltpu.CompilerParams(vmem_limit_bytes=40 * MIB),
        name="forward",
    )(in_hbm(ids), in_hbm(w_router), mine, other, in_hbm(w_up), in_hbm(down))


def grads_kernel(
    chunks, x, gs, hidden, dpre, up_out, down_out, up_buf, down_buf, sems
):
    rows, width = x.shape
    ff = hidden.shape[1]
    kc, fc = width // chunks, ff // chunks
    copies = []
    for i in range(chunks):
        part = slice(i * fc, (i + 1) * fc)
        down_buf[part, :] = dot(hidden[:, part], gs[...], 0, 0).astype(BF16)
        copies.append(pltpu.make_async_copy(down_buf.at[part], down_out.at[part], sems.at[0, i]))
        copies[-1].start()
        part = slice(i * kc, (i + 1) * kc)
        up_buf[part, :] = dot(x[:, part], dpre[...], 0, 0).astype(BF16)
        copies.append(pltpu.make_async_copy(up_buf.at[part], up_out.at[part], sems.at[1, i]))
        copies[-1].start()
    for c in copies:
        c.wait()


def grads(x, gs, hidden, dpre):
    rows, width = x.shape
    ff = hidden.shape[1]
    chunks = 8 if ff % 1024 == 0 else 1
    return pl.pallas_call(
        functools.partial(grads_kernel, chunks),
        out_shape=(
            jax.ShapeDtypeStruct((width, ff), BF16),
            jax.ShapeDtypeStruct((ff, width), BF16),
        ),
        in_specs=[VM] * 4,
        out_specs=(HBM, HBM),
        scratch_shapes=[
            pltpu.VMEM((width, ff), BF16),
            pltpu.VMEM((ff, width), BF16),
            pltpu.SemaphoreType.DMA((2, chunks)),
        ],
        compiler_params=pltpu.CompilerParams(vmem_limit_bytes=40 * MIB),
        name="grads",
    )(x, gs, hidden, dpre)


def router_kernel(ids, x, terms, router_out):
    rows = x.shape[0]
    half = rows // 2
    core = lax.axis_index("core")
    dl = jnp.sum(terms[...], axis=0)
    experts = router_out.shape[0]
    expert = lax.broadcasted_iota(jnp.int32, (experts, rows), 0)
    dlogit = jnp.where(ids[0:1, :] == expert, dl, 0.0) - jnp.where(ids[1:2, :] == expert, dl, 0.0)
    high = dlogit.astype(BF16)
    rest = dlogit - high.astype(F32)
    mid = rest.astype(BF16)
    low = (rest - mid.astype(F32)).astype(BF16)
    perm = token_of_row(rows, core, (rows, rows), 1) == lax.broadcasted_iota(jnp.int32, (rows, rows), 0)
    split = dot(jnp.concatenate([low, mid, high], axis=0), perm.astype(BF16)).astype(BF16)
    sums = []
    for part in (slice(0, half), slice(half, rows)):
        s = dot(split[:, part], x[part, :])
        sums.append(s[:experts] + s[experts : 2 * experts] + s[2 * experts :])
    router_out[...] = sums[0] + sums[1]


def router(ids, x, terms, experts):
    return pl.pallas_call(
        router_kernel,
        out_shape=jax.ShapeDtypeStruct((experts, x.shape[1]), F32),
        in_specs=[VM] * 3,
        out_specs=VM,
        compiler_params=pltpu.CompilerParams(vmem_limit_bytes=16 * MIB),
        name="router",
    )(ids, x, terms)


def local(tokens, cotangent, route_ids, w_router, w_up, down_weight):
    chips = lax.axis_size("dp") * lax.axis_size("ey")
    ids = route_ids.T
    mine = lax.all_to_all(pack(tokens, cotangent, chips), CHIPS, 0, 0, tiled=True)
    other = lax.ppermute(mine, "core", [(0, 1), (1, 0)])
    x, gs, hidden, dpre, terms = forward(ids, w_router, mine, other, w_up[0], down_weight[0])
    terms = lax.all_to_all(terms, AXES, 0, 0, tiled=True)
    grad_up, grad_down = grads(x, gs, hidden, dpre)
    grad_router = router(ids, x, terms, w_router.shape[0])
    return (grad_up[None], grad_down[None], grad_router)


def solution(mesh):
    n_data, n_experts = mesh.shape["dp"], mesh.shape["expert"]
    split = Mesh(mesh.devices.reshape(n_data, n_experts // 2, 2), AXES)
    experts = ("ey", "core")
    return jax.shard_map(
        local,
        mesh=split,
        in_specs=(
            P(AXES, None),
            P(AXES, None),
            P(),
            P(),
            P(experts, None, "dp"),
            P(experts, "dp", None),
        ),
        out_specs=(P(experts, None, "dp"), P(experts, "dp", None), P()),
        check_vma=False,
    )
```

time: 57.4 us -> 39.5 us (0.69)
  blocking collectives: 0 us -> 18 us
  starting transfers between devices: 15.5 us -> 2.56 us
  waiting for transfers between devices: 10.4 us -> 2.18 us
  Pallas kernels: 22.6 us -> 15.7 us
  local copies, waits for them, and re-layouts: 6.55 us -> 0.01 us
  other arithmetic: 1.01 us -> 0 us
    all_to_all x0 -> x1, blocking collectives: none -> 18 us  [local(): lax.all_to_all(pack(tokens, cotangent, chips), CHIPS, 0, 0, tiled=True)]
    ppermute x5 -> x1, starting transfers between devices: 9.35 us -> 0.01 us  [local(): other = lax.ppermute(mine, 'core', [(0, 1), (1, 0)])]
    ppermute x5 -> x1, waiting for transfers between devices: 10.4 us -> 1.53 us  [local(): other = lax.ppermute(mine, 'core', [(0, 1), (1, 0)])]
    pallas_call x3 -> x4, Pallas kernels: 22.6 us -> 15.7 us  [the longest x1 7.43 us: forward(): pl.pallas_call(functools.partial(forward_kernel, chunks), out_shape=(pltp...]
    all_to_all x1, starting transfers between devices: 6.16 us -> 2.56 us  [local(): terms = lax.all_to_all(terms, AXES, 0, 0, tiled=True)]
    concatenate x3 -> x0, local copies, waits for them, and re-layouts: 3.16 us -> none  [the longest x2 2.42 us: gather_rows(): row = jnp.concatenate([row, other], axis=0)]
    unnamed x4 -> x2, local copies, waits for them, and re-layouts: 2.69 us -> 0.01 us
    reshape x1 -> x0, local copies, waits for them, and re-layouts: 0.69 us -> none  [local(): row_tok = (jnp.asarray(order, jnp.int32) ^ me).reshape(n, 1)]
  transfers between devices with their start and end apart: 6 -> 2, of which waited for: 4 -> 2; matrix products, arithmetic and copies ran while one was open for 5% -> 0% of each run, Pallas kernels for 15% -> 16%
where the time goes in v2:
time: 39.5 us; the launch traced here: 39.1 us
  blocking collectives  18 us (46%)
  Pallas kernels  15.7 us (40%)
  starting transfers between devices  2.56 us (6%)
  waiting for transfers between devices  2.18 us (6%)
  between operations  0.66 us (2%)
    all_to_all x1, blocking collectives, local(): lax.all_to_all(pack(tokens, cotangent, chips), CHIPS, 0, 0, tiled=True)  18 us
    pallas_call x1, Pallas kernels, forward(): pl.pallas_call(functools.partial(forward_kernel, chunks), out_shape=(pltp...  7.43 us
    pallas_call x1, Pallas kernels, grads(): pl.pallas_call(functools.partial(grads_kernel, chunks), out_shape=(jax.Sh...  6.42 us
    all_to_all x1, starting transfers between devices, local(): terms = lax.all_to_all(terms, AXES, 0, 0, tiled=True)  2.56 us
    ppermute x1, waiting for transfers between devices, local(): other = lax.ppermute(mine, 'core', [(0, 1), (1, 0)])  1.53 us
    pallas_call x1, Pallas kernels, router(): pl.pallas_call(router_kernel, out_shape=jax.ShapeDtypeStruct((experts, x....  1.02 us
    pallas_call x1, Pallas kernels, pack(): pl.pallas_call(pack_kernel, out_shape=pltpu.VMEM((n, 2, tokens.shape[1]),...  0.8 us
  transfers between devices with their start and end apart: 2, of which 2 were waited for; matrix products, arithmetic and copies ran while one was open for 0% of the time, Pallas kernels for 16%

profile of v2, /device:TPU:0, one launch (start us, length us, event | category | flops | bytes accessed | tf_op | source)
XLA Modules:
  0.0 39.1 jit_solution(18216625849108593338)
XLA Ops:
  0.6 0.8 %pack.1 = bf16[16,2,4096]{2,1,0:T(2,128)(2,1)S(1)} custom-call(bf16[1,4096]{1,0:T(2,128)(2,1)} %tokens.1, bf16[1,4096]{1,0:T(2,128)(2,1)} %cotangent.1), custom_call_target="tpu_custom_call" | custom-call | tf_op jit(solution)/shard_map/pack/pallas_call | solution.py:40
  1.4 18.0 %all_to_all.10.mine = bf16[16,2,4096]{2,1,0:T(2,128)(2,1)S(1)} all-to-all(bf16[16,2,4096]{2,1,0:T(2,128)(2,1)S(1)} %pack.1), channel_id=1, replica_groups=mesh['dp'=8,'ey'=2,'core'=2] {'dp','ey'}, dimensions={0} | all-to-all | bytes 524288 | tf_op jit(solution)/shard_map/all_to_all | solution.py:237
  19.4 0.0 collective-permute-start
  19.4 1.5 %collective-permute-done.other = bf16[16,2,4096]{2,1,0:T(2,128)(2,1)S(1)} collective-permute-done((bf16[16,2,4096]{2,1,0:T(2,128)(2,1)S(1)}, bf16[16,2,4096]{2,1,0:T(2,128)(2,1)S(1)}, u32[]{:S(2)}, u32[]{:S(2)}) %collective-permute-start) | collective-permute-done | bytes 262176 | tf_op jit(solution)/shard_map/ppermute | solution.py:238
  21.0 0.0 copy-start
  21.0 7.4 %forward.1 = (bf16[32,4096]{1,0:T(8,128)(2,1)S(1)}, bf16[32,4096]{1,0:T(8,128)(2,1)S(1)}, bf16[32,1024]{1,0:T(8,128)(2,1)S(1)}, bf16[32,1024]{1,0:T(8,128)(2,1)S(1)}, f32[32,1,32]{2,1,0:T(1,128)}) custom-call(s32[2,32]{1,0:T(2,128)} %bitcast.5, bf16[4,4096]{1,0:T(4,128)(2,1)} %gate_in.1, bf16[16,2,4096]{2,1,0:T(2,128)(2,1)S(1)} %all_to_all.10.mine, ...), custom_call_target="tpu_custom_call" | custom-call | tf_op jit(solution)/shard_map/forward/pallas_call | solution.py:137
  28.4 2.6 %all-to-all-start.1 = ((f32[32,1,32]{2,1,0:T(1,128)}), f32[32,1,32]{2,1,0:T(1,128)S(1)}, u32[]{:S(2)}, u32[]{:S(2)}) async-start(f32[32,1,32]{2,1,0:T(1,128)} %get-tuple-element.16), calls=%async_computation.1 | async-start | bytes 32768 | tf_op jit(solution)/shard_map/all_to_all | solution.py:240
  31.0 6.4 %grads.1 = (bf16[4096,1024]{1,0:T(8,128)(2,1)}, bf16[1024,4096]{1,0:T(8,128)(2,1)}) custom-call(bf16[32,4096]{1,0:T(8,128)(2,1)S(1)} %get-tuple-element.10.x, bf16[32,4096]{1,0:T(8,128)(2,1)S(1)} %get-tuple-element.11.gs, bf16[32,1024]{1,0:T(8,128)(2,1)S(1)} %get-tuple-element.12.hidden, bf16[32,1024]{1,0:T(8,128)(2,1)S(1)} %get-tuple-element.13.dpre), custom_call_target="tpu_custom_call" | custom-call | tf_op jit(solution)/shard_map/grads/pallas_call | solution.py:184
  37.4 0.6 %all-to-all-done.1.terms = f32[32,1,32]{2,1,0:T(1,128)S(1)} async-done(((f32[32,1,32]{2,1,0:T(1,128)}), f32[32,1,32]{2,1,0:T(1,128)S(1)}, u32[]{:S(2)}, u32[]{:S(2)}) %all-to-all-start.1) | async-done | bytes 4128 | tf_op jit(solution)/shard_map/all_to_all | solution.py:240
  38.0 0.0 copy-done
  38.0 1.0 %router.1 = f32[4,4096]{1,0:T(4,128)} custom-call(s32[2,32]{1,0:T(2,128)S(1)} %bitcast.6, bf16[32,4096]{1,0:T(8,128)(2,1)S(1)} %get-tuple-element.10.x, f32[32,1,32]{2,1,0:T(1,128)S(1)} %all-to-all-done.1.terms), custom_call_target="tpu_custom_call" | custom-call | tf_op jit(solution)/shard_map/router/pallas_call | solution.py:224
Async XLA Ops:
  19.4 1.5 %collective-permute-start = (bf16[16,2,4096]{2,1,0:T(2,128)(2,1)S(1)}, bf16[16,2,4096]{2,1,0:T(2,128)(2,1)S(1)}, u32[]{:S(2)}, u32[]{:S(2)}) collective-permute-start(bf16[16,2,4096]{2,1,0:T(2,128)(2,1)S(1)} %all_to_all.10.mine), channel_id=1, source_target_pairs={{0,1},{1,0},{2,3},{3,2},{4,5},{5,4},{6,7},{7,6},{8,9},{9,8},{10,11... | collective-permute-start | bytes 786440 | tf_op jit(solution)/shard_map/ppermute | solution.py:238
  21.0 17.1 %copy-start = (s32[32,2]{0,1:T(2,128)S(1)}, s32[32,2]{0,1:T(2,128)}, u32[]{:S(2)}) copy-start(s32[32,2]{0,1:T(2,128)} %param.8) | copy-start | bytes 772
  28.4 9.6 %all-to-all-start.1 = ((f32[32,1,32]{2,1,0:T(1,128)}), f32[32,1,32]{2,1,0:T(1,128)S(1)}, u32[]{:S(2)}, u32[]{:S(2)}) async-start(f32[32,1,32]{2,1,0:T(1,128)} %get-tuple-element.16), calls=%async_computation.1 | async-start | bytes 32768 | tf_op jit(solution)/shard_map/all_to_all | solution.py:240

commit v3 on v2

v3 whole, which is shorter than its diff:
```python
import functools

import jax
import jax.numpy as jnp
from jax import lax
from jax.experimental import pallas as pl
from jax.experimental.pallas import tpu as pltpu
from jax.sharding import Mesh, PartitionSpec as P

F32 = jnp.float32
BF16 = jnp.bfloat16
CHIPS = ("dp", "ey")
AXES = ("dp", "ey", "core")
MIB = 1024 * 1024
VM = pl.BlockSpec(memory_space=pltpu.VMEM)
HBM = pl.BlockSpec(memory_space=pltpu.HBM)


def dot(a, b, ca=1, cb=0):
    return lax.dot_general(a, b, (((ca,), (cb,)), ((), ())), preferred_element_type=F32)


def in_hbm(x):
    return pltpu.with_memory_space_constraint(x, pltpu.HBM)


def pack_kernel(tokens, cotangent, out, buf, sems):
    loads = [
        pltpu.make_async_copy(ref, buf.at[i], sems.at[i]) for i, ref in enumerate((tokens, cotangent))
    ]
    for c in loads:
        c.start()
    for c in loads:
        c.wait()
    out[...] = jnp.concatenate([buf[0], buf[1]], axis=0)[None]


def pack(tokens, cotangent):
    return pl.pallas_call(
        pack_kernel,
        out_shape=pltpu.VMEM((1, 2, tokens.shape[1]), BF16),
        in_specs=[HBM, HBM],
        out_specs=VM,
        scratch_shapes=[pltpu.VMEM((2,) + tokens.shape, BF16), pltpu.SemaphoreType.DMA((2,))],
        compiler_params=pltpu.CompilerParams(vmem_limit_bytes=16 * MIB),
        name="pack",
    )(in_hbm(tokens), in_hbm(cotangent))


def stages(n):
    bits = n.bit_length() - 1
    shifts, high = [], bits
    while high > 1:
        low = max(1, high - 2)
        shifts.append((low, high - low))
        high = low
    return shifts


def spread(blocks, n, shift, count):
    parts = [blocks]
    for step in range(1, 1 << count):
        pairs = [(i, i ^ (step << shift)) for i in range(n)]
        parts.append(lax.ppermute(blocks, AXES, pairs))
    return jnp.concatenate(parts, axis=0)


def prefetch_kernel(count, *refs):
    sources, targets, sems = refs[:count], refs[-1 - count : -1], refs[-1]
    copies = [
        pltpu.make_async_copy(source, target, sems.at[i])
        for i, (source, target) in enumerate(zip(sources, targets))
    ]
    for c in copies:
        c.start()
    if len(refs) > 2 * count + 1:
        held, turned = refs[count], refs[count + 1]
        step = min(256, held.shape[0])
        for i in range(0, held.shape[0], step):
            turned[:, i : i + step] = held[i : i + step, :].T
    for c in copies:
        c.wait()


def prefetch(arrays, held=None):
    extra = [] if held is None else [held]
    turned = [pltpu.VMEM(h.shape[::-1], h.dtype) for h in extra]
    return pl.pallas_call(
        functools.partial(prefetch_kernel, len(arrays)),
        out_shape=tuple(turned) + tuple(pltpu.VMEM(a.shape, a.dtype) for a in arrays),
        in_specs=[HBM] * len(arrays) + [VM] * len(extra),
        out_specs=(VM,) * (len(arrays) + len(extra)),
        scratch_shapes=[pltpu.SemaphoreType.DMA((len(arrays),))],
        compiler_params=pltpu.CompilerParams(vmem_limit_bytes=8 * MIB),
        name="turn" if extra else "prefetch",
    )(*[in_hbm(a) for a in arrays], *extra)


def device_index():
    place = lax.axis_index("dp") * lax.axis_size("ey") + lax.axis_index("ey")
    return 2 * place + lax.axis_index("core")


def token_of_row(rows, shape, dim):
    row = lax.broadcasted_iota(jnp.int32, shape, dim)
    half = rows // 2
    token = jnp.where(row < half, 0, 1) ^ device_index()
    digits = lax.rem(row, half)
    for shift, count in stages(rows):
        token = token ^ ((digits & ((1 << count) - 1)) << shift)
        digits = digits >> count
    return token


def row_dots(x, gate):
    if x.shape[0] > 64:
        return dot(x[...], gate[...], 1, 1)
    sums = []
    for e in range(gate.shape[0]):
        total = jnp.zeros((x.shape[0], 128), F32)
        for k in range(0, x.shape[1], 128):
            part = slice(k, k + 128)
            total = total + x[:, part].astype(F32) * gate[e : e + 1, part].astype(F32)
        sums.append(jnp.sum(total, axis=1, keepdims=True))
    return jnp.concatenate(sums, axis=1)


def gate_values(ids, gate, x):
    rows = x.shape[0]
    place = lax.broadcasted_iota(jnp.int32, (rows, rows), 1)
    perm = token_of_row(rows, (rows, rows), 0) == place
    first = jnp.sum(jnp.where(perm, ids[0:1, :], 0), axis=1, keepdims=True)
    second = jnp.sum(jnp.where(perm, ids[1:2, :], 0), axis=1, keepdims=True)
    logits = row_dots(x, gate)
    columns = lax.broadcasted_iota(jnp.int32, logits.shape, 1)
    l0 = jnp.sum(jnp.where(first == columns, logits, 0.0), axis=1, keepdims=True)
    l1 = jnp.sum(jnp.where(second == columns, logits, 0.0), axis=1, keepdims=True)
    return perm, first, second, jax.nn.sigmoid(l0 - l1), jax.nn.sigmoid(l1 - l0)


def forward_kernel(ids, gate, mine, other, w_up, down_t, x, gs, hidden, dpre, terms):
    rows, width = x.shape
    half = rows // 2
    expert = 2 * lax.axis_index("ey") + lax.axis_index("core")
    x[:half, :] = mine[:, 0, :]
    x[half:, :] = other[:, 0, :]
    perm, first, second, p0, p1 = gate_values(ids, gate, x)
    is0 = first == expert
    is1 = second == expert
    weight = jnp.where(is0, p0, 0.0) + jnp.where(is1, p1, 0.0)
    gs[:half, :] = (weight[:half] * mine[:, 1, :].astype(F32)).astype(BF16)
    gs[half:, :] = (weight[half:] * other[:, 1, :].astype(F32)).astype(BF16)
    pre = dot(x[...], w_up[...])
    back = dot(gs[...], down_t[...])
    sig = jax.nn.sigmoid(pre)
    silu = pre * sig
    hidden[...] = silu.astype(BF16)
    dpre[...] = (back * sig * (1.0 + pre * (1.0 - sig))).astype(BF16)
    q = jnp.sum(silu * back, axis=1, keepdims=True)
    dl = (jnp.where(is0, p1, 0.0) - jnp.where(is1, p0, 0.0)) * q
    line = jnp.sum(jnp.where(perm, dl, 0.0), axis=0, keepdims=True)
    terms[...] = jnp.broadcast_to(line[None], terms.shape)


def forward(ids, gate, mine, other, w_up, down_t):
    rows = 2 * mine.shape[0]
    width, ff = w_up.shape
    return pl.pallas_call(
        forward_kernel,
        out_shape=(
            pltpu.VMEM((rows, width), BF16),
            pltpu.VMEM((rows, width), BF16),
            pltpu.VMEM((rows, ff), BF16),
            pltpu.VMEM((rows, ff), BF16),
            pltpu.VMEM((rows, 1, rows), F32),
        ),
        in_specs=[VM] * 6,
        out_specs=(VM,) * 5,
        compiler_params=pltpu.CompilerParams(vmem_limit_bytes=16 * MIB),
        name="forward",
    )(ids, gate, mine, other, w_up, down_t)


def grads_kernel(
    chunks, x, gs, hidden, dpre, up_out, down_out, ordered, up_buf, down_buf, sems
):
    rows, width = x.shape
    ff = hidden.shape[1]
    kc, fc = width // chunks, ff // chunks
    copies = []
    for i in range(chunks):
        part = slice(i * fc, (i + 1) * fc)
        down_buf[part, :] = dot(hidden[:, part], gs[...], 0, 0).astype(BF16)
        copies.append(pltpu.make_async_copy(down_buf.at[part], down_out.at[part], sems.at[0, i]))
        copies[-1].start()
        part = slice(i * kc, (i + 1) * kc)
        up_buf[part, :] = dot(x[:, part], dpre[...], 0, 0).astype(BF16)
        copies.append(pltpu.make_async_copy(up_buf.at[part], up_out.at[part], sems.at[1, i]))
        copies[-1].start()
    perm = token_of_row(rows, (rows, rows), 1) == lax.broadcasted_iota(jnp.int32, (rows, rows), 0)
    ordered[...] = dot(perm.astype(F32).astype(BF16), x[...]).astype(BF16)
    for c in copies:
        c.wait()


def grads(x, gs, hidden, dpre):
    rows, width = x.shape
    ff = hidden.shape[1]
    chunks = 8 if ff % 1024 == 0 else 1
    return pl.pallas_call(
        functools.partial(grads_kernel, chunks),
        out_shape=(
            jax.ShapeDtypeStruct((width, ff), BF16),
            jax.ShapeDtypeStruct((ff, width), BF16),
            pltpu.VMEM((rows, width), BF16),
        ),
        in_specs=[VM] * 4,
        out_specs=(HBM, HBM, VM),
        scratch_shapes=[
            pltpu.VMEM((width, ff), BF16),
            pltpu.VMEM((ff, width), BF16),
            pltpu.SemaphoreType.DMA((2, chunks)),
        ],
        compiler_params=pltpu.CompilerParams(vmem_limit_bytes=40 * MIB),
        name="grads",
    )(x, gs, hidden, dpre)


def router_kernel(ids, x, terms, router_out):
    rows = x.shape[0]
    dl = jnp.sum(terms[...], axis=0)
    experts = router_out.shape[0]
    expert = lax.broadcasted_iota(jnp.int32, (experts, rows), 0)
    dlogit = jnp.where(ids[0:1, :] == expert, dl, 0.0) - jnp.where(ids[1:2, :] == expert, dl, 0.0)
    high = dlogit.astype(BF16)
    rest = dlogit - high.astype(F32)
    mid = rest.astype(BF16)
    low = (rest - mid.astype(F32)).astype(BF16)
    s = dot(jnp.concatenate([low, mid, high], axis=0), x[...])
    router_out[...] = s[:experts] + s[experts : 2 * experts] + s[2 * experts :]


def router(ids, x, terms, experts):
    return pl.pallas_call(
        router_kernel,
        out_shape=jax.ShapeDtypeStruct((experts, x.shape[1]), F32),
        in_specs=[VM] * 3,
        out_specs=VM,
        compiler_params=pltpu.CompilerParams(vmem_limit_bytes=16 * MIB),
        name="router",
    )(ids, x, terms)


def local(tokens, cotangent, route_ids, w_router, w_up, down_weight):
    n = lax.axis_size("dp") * lax.axis_size("ey") * 2
    rows = pack(tokens, cotangent)
    held = []
    for i, (shift, count) in enumerate(stages(n)):
        rows = spread(rows, n, shift, count)
        if i == 0:
            held = prefetch([down_weight[0]])
        elif i == 1:
            held = prefetch([w_up[0], route_ids.T, w_router], held[0])
        rows, *held = lax.optimization_barrier((rows, *held))
    other = lax.ppermute(rows, "core", [(0, 1), (1, 0)])
    down_t, up, ids, gate = held
    x, gs, hidden, dpre, terms = forward(ids, gate, rows, other, up, down_t)
    terms = lax.all_to_all(terms, AXES, 0, 0, tiled=True)
    grad_up, grad_down, ordered = grads(x, gs, hidden, dpre)
    grad_router = router(ids, ordered, terms, w_router.shape[0])
    return (grad_up[None], grad_down[None], grad_router)


def solution(mesh):
    n_data, n_experts = mesh.shape["dp"], mesh.shape["expert"]
    split = Mesh(mesh.devices.reshape(n_data, n_experts // 2, 2), AXES)
    experts = ("ey", "core")
    return jax.shard_map(
        local,
        mesh=split,
        in_specs=(
            P(AXES, None),
            P(AXES, None),
            P(),
            P(),
            P(experts, None, "dp"),
            P(experts, "dp", None),
        ),
        out_specs=(P(experts, None, "dp"), P(experts, "dp", None), P()),
        check_vma=False,
    )
```

time: 39.5 us -> 38.3 us (0.970)
  blocking collectives: 18 us -> 0 us
  starting transfers between devices: 2.56 us -> 14.5 us
  Pallas kernels: 15.7 us -> 19.1 us
  waiting for transfers between devices: 2.18 us -> 3.08 us
  other arithmetic: 0 us -> 0.5 us
    all_to_all x1 -> x0, blocking collectives: 18 us -> none  [local(): lax.all_to_all(pack(tokens, cotangent, chips), CHIPS, 0, 0, tiled=True)]
    ppermute x1 -> x7, starting transfers between devices: 0.01 us -> 9.38 us  [the longest x6 9.31 us: spread(): parts.append(lax.ppermute(blocks, AXES, pairs))]
    pallas_call x2 -> x4, Pallas kernels: 8.23 us -> 11.8 us  [the longest x2 6.8 us: prefetch(): pl.pallas_call(functools.partial(prefetch_kernel, len(arrays)), out_shape...]
    all_to_all x1, starting transfers between devices: 2.56 us -> 5.12 us  [local(): terms = lax.all_to_all(terms, AXES, 0, 0, tiled=True)]
    ppermute x1 -> x7, waiting for transfers between devices: 1.53 us -> 2.44 us  [the longest x1 1.52 us: local(): other = lax.ppermute(rows, 'core', [(0, 1), (1, 0)])]
    concatenate x0 -> x2, other arithmetic: none -> 0.5 us  [spread(): return jnp.concatenate(parts, axis=0)]
  transfers between devices with their start and end apart: 2 -> 8, of which waited for: 2 -> 4; matrix products, arithmetic and copies ran while one was open for 0% -> 0% of each run, Pallas kernels for 16% -> 35%
where the time goes in v3:
time: 38.3 us; the launch traced here: 37.9 us
  Pallas kernels  19.1 us (50%)
  starting transfers between devices  14.5 us (38%)
  waiting for transfers between devices  3.08 us (8%)
  between operations  0.71 us (2%)
  other arithmetic  0.5 us (1%)
    ppermute x6, starting transfers between devices, spread(): parts.append(lax.ppermute(blocks, AXES, pairs))  9.31 us
    pallas_call x2, Pallas kernels, prefetch(): pl.pallas_call(functools.partial(prefetch_kernel, len(arrays)), out_shape...  6.8 us
    pallas_call x1, Pallas kernels, grads(): pl.pallas_call(functools.partial(grads_kernel, chunks), out_shape=(jax.Sh...  6.42 us
    all_to_all x1, starting transfers between devices, local(): terms = lax.all_to_all(terms, AXES, 0, 0, tiled=True)  5.12 us
    pallas_call x1, Pallas kernels, forward(): pl.pallas_call(forward_kernel, out_shape=(pltpu.VMEM((rows, width), BF16)...  4.23 us
    ppermute x1, waiting for transfers between devices, local(): other = lax.ppermute(rows, 'core', [(0, 1), (1, 0)])  1.52 us
    ppermute x6, waiting for transfers between devices, spread(): parts.append(lax.ppermute(blocks, AXES, pairs))  0.92 us
    pallas_call x1, Pallas kernels, router(): pl.pallas_call(router_kernel, out_shape=jax.ShapeDtypeStruct((experts, x....  0.84 us
  transfers between devices with their start and end apart: 8, of which 4 were waited for; matrix products, arithmetic and copies ran while one was open for 0% of the time, Pallas kernels for 35%

profile of v3, /device:TPU:0, one launch (start us, length us, event | category | flops | bytes accessed | tf_op | source)
XLA Modules:
  0.0 37.9 jit_solution(11574752517932498058)
XLA Ops:
  0.6 0.8 %pack.1 = bf16[1,2,4096]{2,1,0:T(2,128)(2,1)S(1)} custom-call(bf16[1,4096]{1,0:T(2,128)(2,1)} %tokens.1, bf16[1,4096]{1,0:T(2,128)(2,1)} %cotangent.1), custom_call_target="tpu_custom_call" | custom-call | tf_op jit(solution)/shard_map/pack/pallas_call | solution.py:39
  1.4 5.1 %collective-permute-start.2 = (bf16[1,2,4096]{2,1,0:T(2,128)(2,1)S(1)}, bf16[1,2,4096]{2,1,0:T(2,128)(2,1)S(1)}, u32[]{:S(2)}, u32[]{:S(2)}) collective-permute-start(bf16[1,2,4096]{2,1,0:T(2,128)(2,1)S(1)} %pack.1), channel_id=1, source_target_pairs={{0,24},{1,25},{2,26},{3,27},{4,28},{5,29},{6,30},{7,31},{8,16},{9,... | collective-permute-start | bytes 49160 | tf_op jit(solution)/shard_map/ppermute | solution.py:64
  6.5 0.0 collective-permute-start.1
  6.5 0.6 %collective-permute-start = (bf16[1,2,4096]{2,1,0:T(2,128)(2,1)S(1)}, bf16[1,2,4096]{2,1,0:T(2,128)(2,1)S(1)}, u32[]{:S(2)}, u32[]{:S(2)}) collective-permute-start(bf16[1,2,4096]{2,1,0:T(2,128)(2,1)S(1)} %pack.1), channel_id=1, source_target_pairs={{0,8},{1,9},{2,10},{3,11},{4,12},{5,13},{6,14},{7,15},{8,0},{9,1},... | collective-permute-start | bytes 49160 | tf_op jit(solution)/shard_map/ppermute | solution.py:64
  7.2 3.4 %prefetch.1.refs_3_ = bf16[1024,4096]{1,0:T(8,128)(2,1)S(1)} custom-call(bf16[1024,4096]{1,0:T(8,128)(2,1)} %bitcast.5), custom_call_target="tpu_custom_call" | custom-call | tf_op jit(solution)/shard_map/prefetch/pallas_call | solution.py:88
  10.6 0.0 collective-permute-done.2
  10.6 0.6 %collective-permute-done.1 = bf16[1,2,4096]{2,1,0:T(2,128)(2,1)S(1)} collective-permute-done((bf16[1,2,4096]{2,1,0:T(2,128)(2,1)S(1)}, bf16[1,2,4096]{2,1,0:T(2,128)(2,1)S(1)}, u32[]{:S(2)}, u32[]{:S(2)}) %collective-permute-start.1) | collective-permute-done | bytes 16416 | tf_op jit(solution)/shard_map/ppermute | solution.py:64
  11.2 0.0 collective-permute-done
  11.2 0.1 pad_maximum_fusion.1
  11.3 2.5 %collective-permute-start.5 = (bf16[4,2,4096]{2,1,0:T(2,128)(2,1)S(1)}, bf16[4,2,4096]{2,1,0:T(2,128)(2,1)S(1)}, u32[]{:S(2)}, u32[]{:S(2)}) collective-permute-start(bf16[4,2,4096]{2,1,0:T(2,128)(2,1)S(1)} %pad_maximum_fusion.1), channel_id=1, source_target_pairs={{0,6},{1,7},{2,4},{3,5},{4,2},{5,3},{6,0},{7,1},{8,14},{9,15},{10,... | collective-permute-start | bytes 196616 | tf_op jit(solution)/shard_map/ppermute | solution.py:64
  13.8 0.5 %collective-permute-start.4 = (bf16[4,2,4096]{2,1,0:T(2,128)(2,1)S(1)}, bf16[4,2,4096]{2,1,0:T(2,128)(2,1)S(1)}, u32[]{:S(2)}, u32[]{:S(2)}) collective-permute-start(bf16[4,2,4096]{2,1,0:T(2,128)(2,1)S(1)} %pad_maximum_fusion.1), channel_id=1, source_target_pairs={{0,4},{1,5},{2,6},{3,7},{4,0},{5,1},{6,2},{7,3},{8,12},{9,13},{10,... | collective-permute-start | bytes 196616 | tf_op jit(solution)/shard_map/ppermute | solution.py:64
  14.3 0.5 %collective-permute-start.3 = (bf16[4,2,4096]{2,1,0:T(2,128)(2,1)S(1)}, bf16[4,2,4096]{2,1,0:T(2,128)(2,1)S(1)}, u32[]{:S(2)}, u32[]{:S(2)}) collective-permute-start(bf16[4,2,4096]{2,1,0:T(2,128)(2,1)S(1)} %pad_maximum_fusion.1), channel_id=1, source_target_pairs={{0,2},{1,3},{2,0},{3,1},{4,6},{5,7},{6,4},{7,5},{8,10},{9,11},{10,... | collective-permute-start | bytes 196616 | tf_op jit(solution)/shard_map/ppermute | solution.py:64
  14.9 3.4 %turn.1 = (bf16[4096,1024]{1,0:T(8,128)(2,1)S(1)}, bf16[4096,1024]{1,0:T(8,128)(2,1)S(1)}, s32[2,32]{1,0:T(2,128)S(1)}, bf16[4,4096]{1,0:T(4,128)(2,1)S(1)}) custom-call(bf16[4096,1024]{1,0:T(8,128)(2,1)} %bitcast.6, s32[2,32]{1,0:T(2,128)} %bitcast.7, bf16[4,4096]{1,0:T(4,128)(2,1)} %refs_2_.1, bf16[1024,4096]{1,0:T(8,128)(2,1)S(1)} %prefetch.1.refs_3_), custom_call_target="tpu_custom_call" | custom-call | tf_op jit(solution)/shard_map/turn/pallas_call | solution.py:88
  18.3 0.0 collective-permute-done.5
  18.3 0.0 collective-permute-done.4
  18.3 0.3 collective-permute-done.3
  18.6 0.4 %pad_maximum_fusion.mine = bf16[16,2,4096]{2,1,0:T(2,128)(2,1)S(1)} fusion(bf16[4,2,4096]{2,1,0:T(2,128)(2,1)S(1)} %collective-permute-done.5, bf16[4,2,4096]{2,1,0:T(2,128)(2,1)S(1)} %collective-permute-done.4, bf16[4,2,4096]{2,1,0:T(2,128)(2,1)S(1)} %collective-permute-done.3, bf16[4,2,4096]{2,1,0:T(2,128)(2,1)S(1)} %pad_maximum_fusion.1), kind=kLoop, calls=%fused_computation | loop fusion | flops 393216 | bytes 524288 | tf_op jit(solution)/shard_map/concatenate | solution.py:65
  19.0 0.1 collective-permute-start.6
  19.1 1.5 %collective-permute-done.6.other = bf16[16,2,4096]{2,1,0:T(2,128)(2,1)S(1)} collective-permute-done((bf16[16,2,4096]{2,1,0:T(2,128)(2,1)S(1)}, bf16[16,2,4096]{2,1,0:T(2,128)(2,1)S(1)}, u32[]{:S(2)}, u32[]{:S(2)}) %collective-permute-start.6) | collective-permute-done | bytes 262176 | tf_op jit(solution)/shard_map/ppermute | solution.py:265
  20.6 4.2 %forward.1 = (bf16[32,4096]{1,0:T(8,128)(2,1)S(1)}, bf16[32,4096]{1,0:T(8,128)(2,1)S(1)}, bf16[32,1024]{1,0:T(8,128)(2,1)S(1)}, bf16[32,1024]{1,0:T(8,128)(2,1)S(1)}, f32[32,1,32]{2,1,0:T(1,128)}) custom-call(s32[2,32]{1,0:T(2,128)S(1)} %get-tuple-element.28.ids, bf16[4,4096]{1,0:T(4,128)(2,1)S(1)} %get-tuple-element.29.gate, ...), custom_call_target="tpu_custom_call" | custom-call | tf_op jit(solution)/shard_map/forward/pallas_call | solution.py:168
  24.8 5.1 %all-to-all-start = ((f32[32,1,32]{2,1,0:T(1,128)}), f32[32,1,32]{2,1,0:T(1,128)S(1)}, u32[]{:S(2)}, u32[]{:S(2)}) async-start(f32[32,1,32]{2,1,0:T(1,128)} %get-tuple-element.40), calls=%async_computation | async-start | bytes 32768 | tf_op jit(solution)/shard_map/all_to_all | solution.py:268
  30.0 6.4 %grads.1 = (bf16[4096,1024]{1,0:T(8,128)(2,1)}, bf16[1024,4096]{1,0:T(8,128)(2,1)}, bf16[32,4096]{1,0:T(8,128)(2,1)S(1)}) custom-call(bf16[32,4096]{1,0:T(8,128)(2,1)S(1)} %get-tuple-element.33.x, bf16[32,4096]{1,0:T(8,128)(2,1)S(1)} %get-tuple-element.34.gs, bf16[32,1024]{1,0:T(8,128)(2,1)S(1)} %get-tuple-element.35.hidden, ...), custom_call_target="tpu_custom_call" | custom-call | tf_op jit(solution)/shard_map/grads/pallas_call | solution.py:210
  36.4 0.6 %all-to-all-done.terms = f32[32,1,32]{2,1,0:T(1,128)S(1)} async-done(((f32[32,1,32]{2,1,0:T(1,128)}), f32[32,1,32]{2,1,0:T(1,128)S(1)}, u32[]{:S(2)}, u32[]{:S(2)}) %all-to-all-start) | async-done | bytes 4128 | tf_op jit(solution)/shard_map/all_to_all | solution.py:268
  37.0 0.8 %router.1 = f32[4,4096]{1,0:T(4,128)} custom-call(s32[2,32]{1,0:T(2,128)S(1)} %get-tuple-element.28.ids, bf16[32,4096]{1,0:T(8,128)(2,1)S(1)} %get-tuple-element.39.x, f32[32,1,32]{2,1,0:T(1,128)S(1)} %all-to-all-done.terms), custom_call_target="tpu_custom_call" | custom-call | tf_op jit(solution)/shard_map/router/pallas_call | solution.py:244
Async XLA Ops:
  1.4 9.2 %collective-permute-start.2 = (bf16[1,2,4096]{2,1,0:T(2,128)(2,1)S(1)}, bf16[1,2,4096]{2,1,0:T(2,128)(2,1)S(1)}, u32[]{:S(2)}, u32[]{:S(2)}) collective-permute-start(bf16[1,2,4096]{2,1,0:T(2,128)(2,1)S(1)} %pack.1), channel_id=1, source_target_pairs={{0,24},{1,25},{2,26},{3,27},{4,28},{5,29},{6,30},{7,31},{8,16},{9,... | collective-permute-start | bytes 49160 | tf_op jit(solution)/shard_map/ppermute | solution.py:64
  6.5 4.6 %collective-permute-start.1 = (bf16[1,2,4096]{2,1,0:T(2,128)(2,1)S(1)}, bf16[1,2,4096]{2,1,0:T(2,128)(2,1)S(1)}, u32[]{:S(2)}, u32[]{:S(2)}) collective-permute-start(bf16[1,2,4096]{2,1,0:T(2,128)(2,1)S(1)} %pack.1), channel_id=1, source_target_pairs={{0,16},{1,17},{2,18},{3,19},{4,20},{5,21},{6,22},{7,23},{8,24},{9,... | collective-permute-start | bytes 49160 | tf_op jit(solution)/shard_map/ppermute | solution.py:64
  6.5 4.6 %collective-permute-start = (bf16[1,2,4096]{2,1,0:T(2,128)(2,1)S(1)}, bf16[1,2,4096]{2,1,0:T(2,128)(2,1)S(1)}, u32[]{:S(2)}, u32[]{:S(2)}) collective-permute-start(bf16[1,2,4096]{2,1,0:T(2,128)(2,1)S(1)} %pack.1), channel_id=1, source_target_pairs={{0,8},{1,9},{2,10},{3,11},{4,12},{5,13},{6,14},{7,15},{8,0},{9,1},... | collective-permute-start | bytes 49160 | tf_op jit(solution)/shard_map/ppermute | solution.py:64
  11.3 7.0 %collective-permute-start.5 = (bf16[4,2,4096]{2,1,0:T(2,128)(2,1)S(1)}, bf16[4,2,4096]{2,1,0:T(2,128)(2,1)S(1)}, u32[]{:S(2)}, u32[]{:S(2)}) collective-permute-start(bf16[4,2,4096]{2,1,0:T(2,128)(2,1)S(1)} %pad_maximum_fusion.1), channel_id=1, source_target_pairs={{0,6},{1,7},{2,4},{3,5},{4,2},{5,3},{6,0},{7,1},{8,14},{9,15},{10,... | collective-permute-start | bytes 196616 | tf_op jit(solution)/shard_map/ppermute | solution.py:64
  13.8 4.5 %collective-permute-start.4 = (bf16[4,2,4096]{2,1,0:T(2,128)(2,1)S(1)}, bf16[4,2,4096]{2,1,0:T(2,128)(2,1)S(1)}, u32[]{:S(2)}, u32[]{:S(2)}) collective-permute-start(bf16[4,2,4096]{2,1,0:T(2,128)(2,1)S(1)} %pad_maximum_fusion.1), channel_id=1, source_target_pairs={{0,4},{1,5},{2,6},{3,7},{4,0},{5,1},{6,2},{7,3},{8,12},{9,13},{10,... | collective-permute-start | bytes 196616 | tf_op jit(solution)/shard_map/ppermute | solution.py:64
  14.3 4.3 %collective-permute-start.3 = (bf16[4,2,4096]{2,1,0:T(2,128)(2,1)S(1)}, bf16[4,2,4096]{2,1,0:T(2,128)(2,1)S(1)}, u32[]{:S(2)}, u32[]{:S(2)}) collective-permute-start(bf16[4,2,4096]{2,1,0:T(2,128)(2,1)S(1)} %pad_maximum_fusion.1), channel_id=1, source_target_pairs={{0,2},{1,3},{2,0},{3,1},{4,6},{5,7},{6,4},{7,5},{8,10},{9,11},{10,... | collective-permute-start | bytes 196616 | tf_op jit(solution)/shard_map/ppermute | solution.py:64
  19.0 1.6 %collective-permute-start.6 = (bf16[16,2,4096]{2,1,0:T(2,128)(2,1)S(1)}, bf16[16,2,4096]{2,1,0:T(2,128)(2,1)S(1)}, u32[]{:S(2)}, u32[]{:S(2)}) collective-permute-start(bf16[16,2,4096]{2,1,0:T(2,128)(2,1)S(1)} %pad_maximum_fusion.mine), channel_id=1, source_target_pairs={{0,1},{1,0},{2,3},{3,2},{4,5},{5,4},{6,7},{7,6},{8,9},{9,8},{10,11... | collective-permute-start | bytes 786440 | tf_op jit(solution)/shard_map/ppermute | solution.py:265
  24.8 12.2 %all-to-all-start = ((f32[32,1,32]{2,1,0:T(1,128)}), f32[32,1,32]{2,1,0:T(1,128)S(1)}, u32[]{:S(2)}, u32[]{:S(2)}) async-start(f32[32,1,32]{2,1,0:T(1,128)} %get-tuple-element.40), calls=%async_computation | async-start | bytes 32768 | tf_op jit(solution)/shard_map/all_to_all | solution.py:268

commit v4 on v3

--- a/solution.py
+++ b/solution.py
@@ -112,26 +112,13 @@
     return token
 
 
-def row_dots(x, gate):
-    if x.shape[0] > 64:
-        return dot(x[...], gate[...], 1, 1)
-    sums = []
-    for e in range(gate.shape[0]):
-        total = jnp.zeros((x.shape[0], 128), F32)
-        for k in range(0, x.shape[1], 128):
-            part = slice(k, k + 128)
-            total = total + x[:, part].astype(F32) * gate[e : e + 1, part].astype(F32)
-        sums.append(jnp.sum(total, axis=1, keepdims=True))
-    return jnp.concatenate(sums, axis=1)
-
-
 def gate_values(ids, gate, x):
     rows = x.shape[0]
     place = lax.broadcasted_iota(jnp.int32, (rows, rows), 1)
     perm = token_of_row(rows, (rows, rows), 0) == place
     first = jnp.sum(jnp.where(perm, ids[0:1, :], 0), axis=1, keepdims=True)
     second = jnp.sum(jnp.where(perm, ids[1:2, :], 0), axis=1, keepdims=True)
-    logits = row_dots(x, gate)
+    logits = dot(x[...], gate[...], 1, 1)
     columns = lax.broadcasted_iota(jnp.int32, logits.shape, 1)
     l0 = jnp.sum(jnp.where(first == columns, logits, 0.0), axis=1, keepdims=True)
     l1 = jnp.sum(jnp.where(second == columns, logits, 0.0), axis=1, keepdims=True)
@@ -140,18 +127,23 @@
 
 def forward_kernel(ids, gate, mine, other, w_up, down_t, x, gs, hidden, dpre, terms):
     rows, width = x.shape
-    half = rows // 2
     expert = 2 * lax.axis_index("ey") + lax.axis_index("core")
-    x[:half, :] = mine[:, 0, :]
-    x[half:, :] = other[:, 0, :]
+    pre = jnp.zeros((rows, w_up.shape[1]), F32)
+    back = jnp.zeros((rows, w_up.shape[1]), F32)
+    step = min(256, width)
+    for k in range(0, width, step):
+        part = slice(k, k + step)
+        x[:, part] = jnp.concatenate([mine[:, 0, part], other[:, 0, part]], axis=0)
+        g = jnp.concatenate([mine[:, 1, part], other[:, 1, part]], axis=0)
+        pre = pre + dot(x[:, part], w_up[part, :])
+        gs[:, part] = g
+        back = back + dot(g, down_t[part, :])
     perm, first, second, p0, p1 = gate_values(ids, gate, x)
     is0 = first == expert
     is1 = second == expert
     weight = jnp.where(is0, p0, 0.0) + jnp.where(is1, p1, 0.0)
-    gs[:half, :] = (weight[:half] * mine[:, 1, :].astype(F32)).astype(BF16)
-    gs[half:, :] = (weight[half:] * other[:, 1, :].astype(F32)).astype(BF16)
-    pre = dot(x[...], w_up[...])
-    back = dot(gs[...], down_t[...])
+    back = weight * back
+    gs[...] = (weight * gs[...].astype(F32)).astype(BF16)
     sig = jax.nn.sigmoid(pre)
     silu = pre * sig
     hidden[...] = silu.astype(BF16)

time: 38.3 us -> 37.5 us (0.979)
  Pallas kernels: 19.1 us -> 18.3 us
    pallas_call x1, Pallas kernels: 4.23 us -> 3.44 us  [forward(): pl.pallas_call(forward_kernel, out_shape=(pltpu.VMEM((rows, width), BF16)...]
  transfers between devices with their start and end apart: 8 -> 8, of which waited for: 4 -> 4; matrix products, arithmetic and copies ran while one was open for 0% -> 0% of each run, Pallas kernels for 35% -> 36%
where the time goes in v4:
time: 37.5 us; the launch traced here: 37.1 us
  Pallas kernels  18.3 us (49%)
  starting transfers between devices  14.5 us (39%)
  waiting for transfers between devices  3.09 us (8%)
  between operations  0.71 us (2%)
  other arithmetic  0.5 us (1%)
    ppermute x6, starting transfers between devices, spread(): parts.append(lax.ppermute(blocks, AXES, pairs))  9.31 us
    pallas_call x2, Pallas kernels, prefetch(): pl.pallas_call(functools.partial(prefetch_kernel, len(arrays)), out_shape...  6.8 us
    pallas_call x1, Pallas kernels, grads(): pl.pallas_call(functools.partial(grads_kernel, chunks), out_shape=(jax.Sh...  6.42 us
    all_to_all x1, starting transfers between devices, local(): terms = lax.all_to_all(terms, AXES, 0, 0, tiled=True)  5.12 us
    pallas_call x1, Pallas kernels, forward(): pl.pallas_call(forward_kernel, out_shape=(pltpu.VMEM((rows, width), BF16)...  3.44 us
    ppermute x1, waiting for transfers between devices, local(): other = lax.ppermute(rows, 'core', [(0, 1), (1, 0)])  1.52 us
    ppermute x6, waiting for transfers between devices, spread(): parts.append(lax.ppermute(blocks, AXES, pairs))  0.92 us
    pallas_call x1, Pallas kernels, router(): pl.pallas_call(router_kernel, out_shape=jax.ShapeDtypeStruct((experts, x....  0.84 us
  transfers between devices with their start and end apart: 8, of which 4 were waited for; matrix products, arithmetic and copies ran while one was open for 0% of the time, Pallas kernels for 36%

profile of v4, /device:TPU:0, one launch (start us, length us, event | category | flops | bytes accessed | tf_op | source)
XLA Modules:
  0.0 37.1 jit_solution(4178005911700823106)
XLA Ops:
  0.6 0.8 %pack.1 = bf16[1,2,4096]{2,1,0:T(2,128)(2,1)S(1)} custom-call(bf16[1,4096]{1,0:T(2,128)(2,1)} %tokens.1, bf16[1,4096]{1,0:T(2,128)(2,1)} %cotangent.1), custom_call_target="tpu_custom_call" | custom-call | tf_op jit(solution)/shard_map/pack/pallas_call | solution.py:39
  1.4 5.1 %collective-permute-start.2 = (bf16[1,2,4096]{2,1,0:T(2,128)(2,1)S(1)}, bf16[1,2,4096]{2,1,0:T(2,128)(2,1)S(1)}, u32[]{:S(2)}, u32[]{:S(2)}) collective-permute-start(bf16[1,2,4096]{2,1,0:T(2,128)(2,1)S(1)} %pack.1), channel_id=1, source_target_pairs={{0,24},{1,25},{2,26},{3,27},{4,28},{5,29},{6,30},{7,31},{8,16},{9,... | collective-permute-start | bytes 49160 | tf_op jit(solution)/shard_map/ppermute | solution.py:64
  6.5 0.0 collective-permute-start.1
  6.5 0.6 %collective-permute-start = (bf16[1,2,4096]{2,1,0:T(2,128)(2,1)S(1)}, bf16[1,2,4096]{2,1,0:T(2,128)(2,1)S(1)}, u32[]{:S(2)}, u32[]{:S(2)}) collective-permute-start(bf16[1,2,4096]{2,1,0:T(2,128)(2,1)S(1)} %pack.1), channel_id=1, source_target_pairs={{0,8},{1,9},{2,10},{3,11},{4,12},{5,13},{6,14},{7,15},{8,0},{9,1},... | collective-permute-start | bytes 49160 | tf_op jit(solution)/shard_map/ppermute | solution.py:64
  7.2 3.4 %prefetch.1.refs_3_ = bf16[1024,4096]{1,0:T(8,128)(2,1)S(1)} custom-call(bf16[1024,4096]{1,0:T(8,128)(2,1)} %bitcast.5), custom_call_target="tpu_custom_call" | custom-call | tf_op jit(solution)/shard_map/prefetch/pallas_call | solution.py:88
  10.6 0.0 collective-permute-done.2
  10.6 0.6 %collective-permute-done.1 = bf16[1,2,4096]{2,1,0:T(2,128)(2,1)S(1)} collective-permute-done((bf16[1,2,4096]{2,1,0:T(2,128)(2,1)S(1)}, bf16[1,2,4096]{2,1,0:T(2,128)(2,1)S(1)}, u32[]{:S(2)}, u32[]{:S(2)}) %collective-permute-start.1) | collective-permute-done | bytes 16416 | tf_op jit(solution)/shard_map/ppermute | solution.py:64
  11.2 0.0 collective-permute-done
  11.2 0.1 pad_maximum_fusion.1
  11.3 2.5 %collective-permute-start.5 = (bf16[4,2,4096]{2,1,0:T(2,128)(2,1)S(1)}, bf16[4,2,4096]{2,1,0:T(2,128)(2,1)S(1)}, u32[]{:S(2)}, u32[]{:S(2)}) collective-permute-start(bf16[4,2,4096]{2,1,0:T(2,128)(2,1)S(1)} %pad_maximum_fusion.1), channel_id=1, source_target_pairs={{0,6},{1,7},{2,4},{3,5},{4,2},{5,3},{6,0},{7,1},{8,14},{9,15},{10,... | collective-permute-start | bytes 196616 | tf_op jit(solution)/shard_map/ppermute | solution.py:64
  13.8 0.5 %collective-permute-start.4 = (bf16[4,2,4096]{2,1,0:T(2,128)(2,1)S(1)}, bf16[4,2,4096]{2,1,0:T(2,128)(2,1)S(1)}, u32[]{:S(2)}, u32[]{:S(2)}) collective-permute-start(bf16[4,2,4096]{2,1,0:T(2,128)(2,1)S(1)} %pad_maximum_fusion.1), channel_id=1, source_target_pairs={{0,4},{1,5},{2,6},{3,7},{4,0},{5,1},{6,2},{7,3},{8,12},{9,13},{10,... | collective-permute-start | bytes 196616 | tf_op jit(solution)/shard_map/ppermute | solution.py:64
  14.3 0.5 %collective-permute-start.3 = (bf16[4,2,4096]{2,1,0:T(2,128)(2,1)S(1)}, bf16[4,2,4096]{2,1,0:T(2,128)(2,1)S(1)}, u32[]{:S(2)}, u32[]{:S(2)}) collective-permute-start(bf16[4,2,4096]{2,1,0:T(2,128)(2,1)S(1)} %pad_maximum_fusion.1), channel_id=1, source_target_pairs={{0,2},{1,3},{2,0},{3,1},{4,6},{5,7},{6,4},{7,5},{8,10},{9,11},{10,... | collective-permute-start | bytes 196616 | tf_op jit(solution)/shard_map/ppermute | solution.py:64
  14.9 3.4 %turn.1 = (bf16[4096,1024]{1,0:T(8,128)(2,1)S(1)}, bf16[4096,1024]{1,0:T(8,128)(2,1)S(1)}, s32[2,32]{1,0:T(2,128)S(1)}, bf16[4,4096]{1,0:T(4,128)(2,1)S(1)}) custom-call(bf16[4096,1024]{1,0:T(8,128)(2,1)} %bitcast.6, s32[2,32]{1,0:T(2,128)} %bitcast.7, bf16[4,4096]{1,0:T(4,128)(2,1)} %refs_2_.1, bf16[1024,4096]{1,0:T(8,128)(2,1)S(1)} %prefetch.1.refs_3_), custom_call_target="tpu_custom_call" | custom-call | tf_op jit(solution)/shard_map/turn/pallas_call | solution.py:88
  18.3 0.0 collective-permute-done.5
  18.3 0.0 collective-permute-done.4
  18.3 0.3 collective-permute-done.3
  18.6 0.4 %pad_maximum_fusion.mine = bf16[16,2,4096]{2,1,0:T(2,128)(2,1)S(1)} fusion(bf16[4,2,4096]{2,1,0:T(2,128)(2,1)S(1)} %collective-permute-done.5, bf16[4,2,4096]{2,1,0:T(2,128)(2,1)S(1)} %collective-permute-done.4, bf16[4,2,4096]{2,1,0:T(2,128)(2,1)S(1)} %collective-permute-done.3, bf16[4,2,4096]{2,1,0:T(2,128)(2,1)S(1)} %pad_maximum_fusion.1), kind=kLoop, calls=%fused_computation | loop fusion | flops 393216 | bytes 524288 | tf_op jit(solution)/shard_map/concatenate | solution.py:65
  19.0 0.1 collective-permute-start.6
  19.1 1.5 %collective-permute-done.6.other = bf16[16,2,4096]{2,1,0:T(2,128)(2,1)S(1)} collective-permute-done((bf16[16,2,4096]{2,1,0:T(2,128)(2,1)S(1)}, bf16[16,2,4096]{2,1,0:T(2,128)(2,1)S(1)}, u32[]{:S(2)}, u32[]{:S(2)}) %collective-permute-start.6) | collective-permute-done | bytes 262176 | tf_op jit(solution)/shard_map/ppermute | solution.py:257
  20.6 3.4 %forward.1 = (bf16[32,4096]{1,0:T(8,128)(2,1)S(1)}, bf16[32,4096]{1,0:T(8,128)(2,1)S(1)}, bf16[32,1024]{1,0:T(8,128)(2,1)S(1)}, bf16[32,1024]{1,0:T(8,128)(2,1)S(1)}, f32[32,1,32]{2,1,0:T(1,128)}) custom-call(s32[2,32]{1,0:T(2,128)S(1)} %get-tuple-element.28.ids, bf16[4,4096]{1,0:T(4,128)(2,1)S(1)} %get-tuple-element.29.gate, ...), custom_call_target="tpu_custom_call" | custom-call | tf_op jit(solution)/shard_map/forward/pallas_call | solution.py:160
  24.0 5.1 %all-to-all-start = ((f32[32,1,32]{2,1,0:T(1,128)}), f32[32,1,32]{2,1,0:T(1,128)S(1)}, u32[]{:S(2)}, u32[]{:S(2)}) async-start(f32[32,1,32]{2,1,0:T(1,128)} %get-tuple-element.40), calls=%async_computation | async-start | bytes 32768 | tf_op jit(solution)/shard_map/all_to_all | solution.py:260
  29.2 6.4 %grads.1 = (bf16[4096,1024]{1,0:T(8,128)(2,1)}, bf16[1024,4096]{1,0:T(8,128)(2,1)}, bf16[32,4096]{1,0:T(8,128)(2,1)S(1)}) custom-call(bf16[32,4096]{1,0:T(8,128)(2,1)S(1)} %get-tuple-element.33.x, bf16[32,4096]{1,0:T(8,128)(2,1)S(1)} %get-tuple-element.34.gs, bf16[32,1024]{1,0:T(8,128)(2,1)S(1)} %get-tuple-element.35.hidden, ...), custom_call_target="tpu_custom_call" | custom-call | tf_op jit(solution)/shard_map/grads/pallas_call | solution.py:202
  35.6 0.6 %all-to-all-done.terms = f32[32,1,32]{2,1,0:T(1,128)S(1)} async-done(((f32[32,1,32]{2,1,0:T(1,128)}), f32[32,1,32]{2,1,0:T(1,128)S(1)}, u32[]{:S(2)}, u32[]{:S(2)}) %all-to-all-start) | async-done | bytes 4128 | tf_op jit(solution)/shard_map/all_to_all | solution.py:260
  36.2 0.8 %router.1 = f32[4,4096]{1,0:T(4,128)} custom-call(s32[2,32]{1,0:T(2,128)S(1)} %get-tuple-element.28.ids, bf16[32,4096]{1,0:T(8,128)(2,1)S(1)} %get-tuple-element.39.x, f32[32,1,32]{2,1,0:T(1,128)S(1)} %all-to-all-done.terms), custom_call_target="tpu_custom_call" | custom-call | tf_op jit(solution)/shard_map/router/pallas_call | solution.py:236
Async XLA Ops:
  1.4 9.2 %collective-permute-start.2 = (bf16[1,2,4096]{2,1,0:T(2,128)(2,1)S(1)}, bf16[1,2,4096]{2,1,0:T(2,128)(2,1)S(1)}, u32[]{:S(2)}, u32[]{:S(2)}) collective-permute-start(bf16[1,2,4096]{2,1,0:T(2,128)(2,1)S(1)} %pack.1), channel_id=1, source_target_pairs={{0,24},{1,25},{2,26},{3,27},{4,28},{5,29},{6,30},{7,31},{8,16},{9,... | collective-permute-start | bytes 49160 | tf_op jit(solution)/shard_map/ppermute | solution.py:64
  6.5 4.6 %collective-permute-start.1 = (bf16[1,2,4096]{2,1,0:T(2,128)(2,1)S(1)}, bf16[1,2,4096]{2,1,0:T(2,128)(2,1)S(1)}, u32[]{:S(2)}, u32[]{:S(2)}) collective-permute-start(bf16[1,2,4096]{2,1,0:T(2,128)(2,1)S(1)} %pack.1), channel_id=1, source_target_pairs={{0,16},{1,17},{2,18},{3,19},{4,20},{5,21},{6,22},{7,23},{8,24},{9,... | collective-permute-start | bytes 49160 | tf_op jit(solution)/shard_map/ppermute | solution.py:64
  6.5 4.6 %collective-permute-start = (bf16[1,2,4096]{2,1,0:T(2,128)(2,1)S(1)}, bf16[1,2,4096]{2,1,0:T(2,128)(2,1)S(1)}, u32[]{:S(2)}, u32[]{:S(2)}) collective-permute-start(bf16[1,2,4096]{2,1,0:T(2,128)(2,1)S(1)} %pack.1), channel_id=1, source_target_pairs={{0,8},{1,9},{2,10},{3,11},{4,12},{5,13},{6,14},{7,15},{8,0},{9,1},... | collective-permute-start | bytes 49160 | tf_op jit(solution)/shard_map/ppermute | solution.py:64
  11.3 7.0 %collective-permute-start.5 = (bf16[4,2,4096]{2,1,0:T(2,128)(2,1)S(1)}, bf16[4,2,4096]{2,1,0:T(2,128)(2,1)S(1)}, u32[]{:S(2)}, u32[]{:S(2)}) collective-permute-start(bf16[4,2,4096]{2,1,0:T(2,128)(2,1)S(1)} %pad_maximum_fusion.1), channel_id=1, source_target_pairs={{0,6},{1,7},{2,4},{3,5},{4,2},{5,3},{6,0},{7,1},{8,14},{9,15},{10,... | collective-permute-start | bytes 196616 | tf_op jit(solution)/shard_map/ppermute | solution.py:64
  13.8 4.5 %collective-permute-start.4 = (bf16[4,2,4096]{2,1,0:T(2,128)(2,1)S(1)}, bf16[4,2,4096]{2,1,0:T(2,128)(2,1)S(1)}, u32[]{:S(2)}, u32[]{:S(2)}) collective-permute-start(bf16[4,2,4096]{2,1,0:T(2,128)(2,1)S(1)} %pad_maximum_fusion.1), channel_id=1, source_target_pairs={{0,4},{1,5},{2,6},{3,7},{4,0},{5,1},{6,2},{7,3},{8,12},{9,13},{10,... | collective-permute-start | bytes 196616 | tf_op jit(solution)/shard_map/ppermute | solution.py:64
  14.3 4.3 %collective-permute-start.3 = (bf16[4,2,4096]{2,1,0:T(2,128)(2,1)S(1)}, bf16[4,2,4096]{2,1,0:T(2,128)(2,1)S(1)}, u32[]{:S(2)}, u32[]{:S(2)}) collective-permute-start(bf16[4,2,4096]{2,1,0:T(2,128)(2,1)S(1)} %pad_maximum_fusion.1), channel_id=1, source_target_pairs={{0,2},{1,3},{2,0},{3,1},{4,6},{5,7},{6,4},{7,5},{8,10},{9,11},{10,... | collective-permute-start | bytes 196616 | tf_op jit(solution)/shard_map/ppermute | solution.py:64
  19.0 1.6 %collective-permute-start.6 = (bf16[16,2,4096]{2,1,0:T(2,128)(2,1)S(1)}, bf16[16,2,4096]{2,1,0:T(2,128)(2,1)S(1)}, u32[]{:S(2)}, u32[]{:S(2)}) collective-permute-start(bf16[16,2,4096]{2,1,0:T(2,128)(2,1)S(1)} %pad_maximum_fusion.mine), channel_id=1, source_target_pairs={{0,1},{1,0},{2,3},{3,2},{4,5},{5,4},{6,7},{7,6},{8,9},{9,8},{10,11... | collective-permute-start | bytes 786440 | tf_op jit(solution)/shard_map/ppermute | solution.py:257
  24.0 12.2 %all-to-all-start = ((f32[32,1,32]{2,1,0:T(1,128)}), f32[32,1,32]{2,1,0:T(1,128)S(1)}, u32[]{:S(2)}, u32[]{:S(2)}) async-start(f32[32,1,32]{2,1,0:T(1,128)} %get-tuple-element.40), calls=%async_computation | async-start | bytes 32768 | tf_op jit(solution)/shard_map/all_to_all | solution.py:260

commit v5 on v4

--- a/solution.py
+++ b/solution.py
@@ -59,17 +59,17 @@
 
 def spread(blocks, n, shift, count):
     parts = [blocks]
-    for step in range(1, 1 << count):
+    for step in range((1 << count) - 1, 0, -1):
         pairs = [(i, i ^ (step << shift)) for i in range(n)]
         parts.append(lax.ppermute(blocks, AXES, pairs))
     return jnp.concatenate(parts, axis=0)
 
 
-def prefetch_kernel(count, *refs):
+def prefetch_kernel(count, spans, *refs):
     sources, targets, sems = refs[:count], refs[-1 - count : -1], refs[-1]
     copies = [
-        pltpu.make_async_copy(source, target, sems.at[i])
-        for i, (source, target) in enumerate(zip(sources, targets))
+        pltpu.make_async_copy(source if span is None else source.at[pl.ds(*span)], target, sems.at[i])
+        for i, (source, span, target) in enumerate(zip(sources, spans, targets))
     ]
     for c in copies:
         c.start()
@@ -82,12 +82,14 @@
         c.wait()
 
 
-def prefetch(arrays, held=None):
+def prefetch(arrays, held=None, span=None):
     extra = [] if held is None else [held]
+    spans = [span] + [None] * (len(arrays) - 1)
+    shapes = [a.shape if p is None else (p[1],) + a.shape[1:] for a, p in zip(arrays, spans)]
     turned = [pltpu.VMEM(h.shape[::-1], h.dtype) for h in extra]
     return pl.pallas_call(
-        functools.partial(prefetch_kernel, len(arrays)),
-        out_shape=tuple(turned) + tuple(pltpu.VMEM(a.shape, a.dtype) for a in arrays),
+        functools.partial(prefetch_kernel, len(arrays), spans),
+        out_shape=tuple(turned) + tuple(pltpu.VMEM(p, a.dtype) for a, p in zip(arrays, shapes)),
         in_specs=[HBM] * len(arrays) + [VM] * len(extra),
         out_specs=(VM,) * (len(arrays) + len(extra)),
         scratch_shapes=[pltpu.SemaphoreType.DMA((len(arrays),))],
@@ -107,7 +109,7 @@
     token = jnp.where(row < half, 0, 1) ^ device_index()
     digits = lax.rem(row, half)
     for shift, count in stages(rows):
-        token = token ^ ((digits & ((1 << count) - 1)) << shift)
+        token = token ^ ((-digits & ((1 << count) - 1)) << shift)
         digits = digits >> count
     return token
 
@@ -125,17 +127,21 @@
     return perm, first, second, jax.nn.sigmoid(l0 - l1), jax.nn.sigmoid(l1 - l0)
 
 
-def forward_kernel(ids, gate, mine, other, w_up, down_t, x, gs, hidden, dpre, terms):
+def forward_kernel(
+    ids, gate, mine, other, up_head, up_tail, down_t, x, gs, hidden, dpre, terms_out, terms, sem
+):
     rows, width = x.shape
     expert = 2 * lax.axis_index("ey") + lax.axis_index("core")
-    pre = jnp.zeros((rows, w_up.shape[1]), F32)
-    back = jnp.zeros((rows, w_up.shape[1]), F32)
+    head = up_head.shape[0]
+    pre = jnp.zeros((rows, down_t.shape[1]), F32)
+    back = jnp.zeros((rows, down_t.shape[1]), F32)
     step = min(256, width)
     for k in range(0, width, step):
         part = slice(k, k + step)
         x[:, part] = jnp.concatenate([mine[:, 0, part], other[:, 0, part]], axis=0)
         g = jnp.concatenate([mine[:, 1, part], other[:, 1, part]], axis=0)
-        pre = pre + dot(x[:, part], w_up[part, :])
+        w_up = up_head[part, :] if k < head else up_tail[k - head : k - head + step, :]
+        pre = pre + dot(x[:, part], w_up)
         gs[:, part] = g
         back = back + dot(g, down_t[part, :])
     perm, first, second, p0, p1 = gate_values(ids, gate, x)
@@ -143,20 +149,23 @@
     is1 = second == expert
     weight = jnp.where(is0, p0, 0.0) + jnp.where(is1, p1, 0.0)
     back = weight * back
-    gs[...] = (weight * gs[...].astype(F32)).astype(BF16)
     sig = jax.nn.sigmoid(pre)
     silu = pre * sig
-    hidden[...] = silu.astype(BF16)
-    dpre[...] = (back * sig * (1.0 + pre * (1.0 - sig))).astype(BF16)
     q = jnp.sum(silu * back, axis=1, keepdims=True)
     dl = (jnp.where(is0, p1, 0.0) - jnp.where(is1, p0, 0.0)) * q
     line = jnp.sum(jnp.where(perm, dl, 0.0), axis=0, keepdims=True)
     terms[...] = jnp.broadcast_to(line[None], terms.shape)
-
-
-def forward(ids, gate, mine, other, w_up, down_t):
+    copy = pltpu.make_async_copy(terms, terms_out, sem)
+    copy.start()
+    gs[...] = (weight * gs[...].astype(F32)).astype(BF16)
+    hidden[...] = silu.astype(BF16)
+    dpre[...] = (back * sig * (1.0 + pre * (1.0 - sig))).astype(BF16)
+    copy.wait()
+
+
+def forward(ids, gate, mine, other, up_head, up_tail, down_t):
     rows = 2 * mine.shape[0]
-    width, ff = w_up.shape
+    width, ff = down_t.shape
     return pl.pallas_call(
         forward_kernel,
         out_shape=(
@@ -164,13 +173,14 @@
             pltpu.VMEM((rows, width), BF16),
             pltpu.VMEM((rows, ff), BF16),
             pltpu.VMEM((rows, ff), BF16),
-            pltpu.VMEM((rows, 1, rows), F32),
+            pltpu.HBM((rows, 1, rows), F32),
         ),
-        in_specs=[VM] * 6,
-        out_specs=(VM,) * 5,
+        in_specs=[VM] * 7,
+        out_specs=(VM,) * 4 + (HBM,),
+        scratch_shapes=[pltpu.VMEM((rows, 1, rows), F32), pltpu.SemaphoreType.DMA],
         compiler_params=pltpu.CompilerParams(vmem_limit_bytes=16 * MIB),
         name="forward",
-    )(ids, gate, mine, other, w_up, down_t)
+    )(ids, gate, mine, other, up_head, up_tail, down_t)
 
 
 def grads_kernel(
@@ -246,17 +256,20 @@
 def local(tokens, cotangent, route_ids, w_router, w_up, down_weight):
     n = lax.axis_size("dp") * lax.axis_size("ey") * 2
     rows = pack(tokens, cotangent)
+    width = tokens.shape[1]
+    head = 3 * width // 4
     held = []
     for i, (shift, count) in enumerate(stages(n)):
         rows = spread(rows, n, shift, count)
         if i == 0:
             held = prefetch([down_weight[0]])
         elif i == 1:
-            held = prefetch([w_up[0], route_ids.T, w_router], held[0])
+            held = prefetch([w_up[0], route_ids.T, w_router], held[0], (0, head))
         rows, *held = lax.optimization_barrier((rows, *held))
     other = lax.ppermute(rows, "core", [(0, 1), (1, 0)])
     down_t, up, ids, gate = held
-    x, gs, hidden, dpre, terms = forward(ids, gate, rows, other, up, down_t)
+    (tail,) = prefetch([w_up[0]], None, (head, width - head))
+    x, gs, hidden, dpre, terms = forward(ids, gate, rows, other, up, tail, down_t)
     terms = lax.all_to_all(terms, AXES, 0, 0, tiled=True)
     grad_up, grad_down, ordered = grads(x, gs, hidden, dpre)
     grad_router = router(ids, ordered, terms, w_router.shape[0])

time: 37.5 us -> 37 us (0.987)
  waiting for transfers between devices: 3.09 us -> 2.17 us
  Pallas kernels: 18.3 us -> 19.2 us
  starting transfers between devices: 14.5 us -> 14 us
    ppermute x1, waiting for transfers between devices: 1.52 us -> 0.01 us  [local(): other = lax.ppermute(rows, 'core', [(0, 1), (1, 0)])]
    pallas_call x2 -> x3, Pallas kernels: 6.8 us -> 7.81 us  [prefetch(): pl.pallas_call(functools.partial(prefetch_kernel, len(arrays), spans), ou...]
    ppermute x6, waiting for transfers between devices: 0.92 us -> 1.52 us  [spread(): parts.append(lax.ppermute(blocks, AXES, pairs))]
    all_to_all x1, starting transfers between devices: 5.12 us -> 4.63 us  [local(): terms = lax.all_to_all(terms, AXES, 0, 0, tiled=True)]
  transfers between devices with their start and end apart: 8 -> 8, of which waited for: 4 -> 4; matrix products, arithmetic and copies ran while one was open for 0% -> 0% of each run, Pallas kernels for 36% -> 39%
where the time goes in v5:
time: 37 us; the launch traced here: 36.7 us
  Pallas kernels  19.2 us (52%)
  starting transfers between devices  14 us (38%)
  waiting for transfers between devices  2.17 us (6%)
  between operations  0.73 us (2%)
  other arithmetic  0.5 us (1%)
    ppermute x6, starting transfers between devices, spread(): parts.append(lax.ppermute(blocks, AXES, pairs))  9.31 us
    pallas_call x3, Pallas kernels, prefetch(): pl.pallas_call(functools.partial(prefetch_kernel, len(arrays), spans), ou...  7.81 us
    pallas_call x1, Pallas kernels, grads(): pl.pallas_call(functools.partial(grads_kernel, chunks), out_shape=(jax.Sh...  6.42 us
    all_to_all x1, starting transfers between devices, local(): terms = lax.all_to_all(terms, AXES, 0, 0, tiled=True)  4.63 us
    pallas_call x1, Pallas kernels, forward(): pl.pallas_call(forward_kernel, out_shape=(pltpu.VMEM((rows, width), BF16)...  3.4 us
    ppermute x6, waiting for transfers between devices, spread(): parts.append(lax.ppermute(blocks, AXES, pairs))  1.52 us
    pallas_call x1, Pallas kernels, router(): pl.pallas_call(router_kernel, out_shape=jax.ShapeDtypeStruct((experts, x....  0.84 us
    pallas_call x1, Pallas kernels, pack(): pl.pallas_call(pack_kernel, out_shape=pltpu.VMEM((1, 2, tokens.shape[1]),...  0.79 us
  transfers between devices with their start and end apart: 8, of which 4 were waited for; matrix products, arithmetic and copies ran while one was open for 0% of the time, Pallas kernels for 39%

profile of v5, /device:TPU:0, one launch (start us, length us, event | category | flops | bytes accessed | tf_op | source)
XLA Modules:
  0.0 36.7 jit_solution(4192358580607090315)
XLA Ops:
  0.6 0.8 %pack.1 = bf16[1,2,4096]{2,1,0:T(2,128)(2,1)S(1)} custom-call(bf16[1,4096]{1,0:T(2,128)(2,1)} %tokens.1, bf16[1,4096]{1,0:T(2,128)(2,1)} %cotangent.1), custom_call_target="tpu_custom_call" | custom-call | tf_op jit(solution)/shard_map/pack/pallas_call | solution.py:39
  1.4 5.1 %collective-permute-start = (bf16[1,2,4096]{2,1,0:T(2,128)(2,1)S(1)}, bf16[1,2,4096]{2,1,0:T(2,128)(2,1)S(1)}, u32[]{:S(2)}, u32[]{:S(2)}) collective-permute-start(bf16[1,2,4096]{2,1,0:T(2,128)(2,1)S(1)} %pack.1), channel_id=1, source_target_pairs={{0,24},{1,25},{2,26},{3,27},{4,28},{5,29},{6,30},{7,31},{8,16},{9,... | collective-permute-start | bytes 49160 | tf_op jit(solution)/shard_map/ppermute | solution.py:64
  6.5 0.0 collective-permute-start.1
  6.5 0.6 %collective-permute-start.2 = (bf16[1,2,4096]{2,1,0:T(2,128)(2,1)S(1)}, bf16[1,2,4096]{2,1,0:T(2,128)(2,1)S(1)}, u32[]{:S(2)}, u32[]{:S(2)}) collective-permute-start(bf16[1,2,4096]{2,1,0:T(2,128)(2,1)S(1)} %pack.1), channel_id=1, source_target_pairs={{0,8},{1,9},{2,10},{3,11},{4,12},{5,13},{6,14},{7,15},{8,0},{9,1},... | collective-permute-start | bytes 49160 | tf_op jit(solution)/shard_map/ppermute | solution.py:64
  7.2 3.4 %prefetch.2.refs_3_ = bf16[1024,4096]{1,0:T(8,128)(2,1)S(1)} custom-call(bf16[1024,4096]{1,0:T(8,128)(2,1)} %bitcast.7), custom_call_target="tpu_custom_call" | custom-call | tf_op jit(solution)/shard_map/prefetch/pallas_call | solution.py:90
  10.6 0.0 collective-permute-done
  10.6 0.6 %collective-permute-done.1 = bf16[1,2,4096]{2,1,0:T(2,128)(2,1)S(1)} collective-permute-done((bf16[1,2,4096]{2,1,0:T(2,128)(2,1)S(1)}, bf16[1,2,4096]{2,1,0:T(2,128)(2,1)S(1)}, u32[]{:S(2)}, u32[]{:S(2)}) %collective-permute-start.1) | collective-permute-done | bytes 16416 | tf_op jit(solution)/shard_map/ppermute | solution.py:64
  11.2 0.0 collective-permute-done.2
  11.2 0.1 pad_maximum_fusion.1
  11.3 2.5 %collective-permute-start.3 = (bf16[4,2,4096]{2,1,0:T(2,128)(2,1)S(1)}, bf16[4,2,4096]{2,1,0:T(2,128)(2,1)S(1)}, u32[]{:S(2)}, u32[]{:S(2)}) collective-permute-start(bf16[4,2,4096]{2,1,0:T(2,128)(2,1)S(1)} %pad_maximum_fusion.1), channel_id=1, source_target_pairs={{0,6},{1,7},{2,4},{3,5},{4,2},{5,3},{6,0},{7,1},{8,14},{9,15},{10,... | collective-permute-start | bytes 196616 | tf_op jit(solution)/shard_map/ppermute | solution.py:64
  13.8 0.5 %collective-permute-start.4 = (bf16[4,2,4096]{2,1,0:T(2,128)(2,1)S(1)}, bf16[4,2,4096]{2,1,0:T(2,128)(2,1)S(1)}, u32[]{:S(2)}, u32[]{:S(2)}) collective-permute-start(bf16[4,2,4096]{2,1,0:T(2,128)(2,1)S(1)} %pad_maximum_fusion.1), channel_id=1, source_target_pairs={{0,4},{1,5},{2,6},{3,7},{4,0},{5,1},{6,2},{7,3},{8,12},{9,13},{10,... | collective-permute-start | bytes 196616 | tf_op jit(solution)/shard_map/ppermute | solution.py:64
  14.3 0.5 %collective-permute-start.5 = (bf16[4,2,4096]{2,1,0:T(2,128)(2,1)S(1)}, bf16[4,2,4096]{2,1,0:T(2,128)(2,1)S(1)}, u32[]{:S(2)}, u32[]{:S(2)}) collective-permute-start(bf16[4,2,4096]{2,1,0:T(2,128)(2,1)S(1)} %pad_maximum_fusion.1), channel_id=1, source_target_pairs={{0,2},{1,3},{2,0},{3,1},{4,6},{5,7},{6,4},{7,5},{8,10},{9,11},{10,... | collective-permute-start | bytes 196616 | tf_op jit(solution)/shard_map/ppermute | solution.py:64
  14.9 2.8 %turn.1 = (bf16[4096,1024]{1,0:T(8,128)(2,1)S(1)}, bf16[3072,1024]{1,0:T(8,128)(2,1)S(1)}, s32[2,32]{1,0:T(2,128)S(1)}, bf16[4,4096]{1,0:T(4,128)(2,1)S(1)}) custom-call(bf16[4096,1024]{1,0:T(8,128)(2,1)} %bitcast.5, s32[2,32]{1,0:T(2,128)} %bitcast.8, bf16[4,4096]{1,0:T(4,128)(2,1)} %refs_2_.1, bf16[1024,4096]{1,0:T(8,128)(2,1)S(1)} %prefetch.2.refs_3_), custom_call_target="tpu_custom_call" | custom-call | tf_op jit(solution)/shard_map/turn/pallas_call | solution.py:90
  17.7 0.0 collective-permute-done.3
  17.7 0.4 %collective-permute-done.4 = bf16[4,2,4096]{2,1,0:T(2,128)(2,1)S(1)} collective-permute-done((bf16[4,2,4096]{2,1,0:T(2,128)(2,1)S(1)}, bf16[4,2,4096]{2,1,0:T(2,128)(2,1)S(1)}, u32[]{:S(2)}, u32[]{:S(2)}) %collective-permute-start.4) | collective-permute-done | bytes 65568 | tf_op jit(solution)/shard_map/ppermute | solution.py:64
  18.1 0.5 %collective-permute-done.5 = bf16[4,2,4096]{2,1,0:T(2,128)(2,1)S(1)} collective-permute-done((bf16[4,2,4096]{2,1,0:T(2,128)(2,1)S(1)}, bf16[4,2,4096]{2,1,0:T(2,128)(2,1)S(1)}, u32[]{:S(2)}, u32[]{:S(2)}) %collective-permute-start.5) | collective-permute-done | bytes 65568 | tf_op jit(solution)/shard_map/ppermute | solution.py:64
  18.6 0.4 %pad_maximum_fusion.mine = bf16[16,2,4096]{2,1,0:T(2,128)(2,1)S(1)} fusion(bf16[4,2,4096]{2,1,0:T(2,128)(2,1)S(1)} %collective-permute-done.5, bf16[4,2,4096]{2,1,0:T(2,128)(2,1)S(1)} %collective-permute-done.4, bf16[4,2,4096]{2,1,0:T(2,128)(2,1)S(1)} %collective-permute-done.3, bf16[4,2,4096]{2,1,0:T(2,128)(2,1)S(1)} %pad_maximum_fusion.1), kind=kLoop, calls=%fused_computation | loop fusion | flops 393216 | bytes 524288 | tf_op jit(solution)/shard_map/concatenate | solution.py:65
  19.0 0.1 collective-permute-start.6
  19.1 1.6 %prefetch.3.up_tail = bf16[1024,1024]{1,0:T(8,128)(2,1)S(1)} custom-call(bf16[4096,1024]{1,0:T(8,128)(2,1)} %bitcast.6), custom_call_target="tpu_custom_call" | custom-call | tf_op jit(solution)/shard_map/prefetch/pallas_call | solution.py:90
  20.7 0.0 collective-permute-done.6.other
  20.7 3.4 %forward.1 = (bf16[32,4096]{1,0:T(8,128)(2,1)S(1)}, bf16[32,4096]{1,0:T(8,128)(2,1)S(1)}, bf16[32,1024]{1,0:T(8,128)(2,1)S(1)}, bf16[32,1024]{1,0:T(8,128)(2,1)S(1)}, f32[32,1,32]{2,1,0:T(1,128)}) custom-call(s32[2,32]{1,0:T(2,128)S(1)} %get-tuple-element.28.ids, bf16[4,4096]{1,0:T(4,128)(2,1)S(1)} %get-tuple-element.29.gate, ...), custom_call_target="tpu_custom_call" | custom-call | tf_op jit(solution)/shard_map/forward/pallas_call | solution.py:169
  24.1 4.6 %all-to-all-start = ((f32[32,1,32]{2,1,0:T(1,128)}), f32[32,1,32]{2,1,0:T(1,128)S(1)}, u32[]{:S(2)}, u32[]{:S(2)}) async-start(f32[32,1,32]{2,1,0:T(1,128)} %get-tuple-element.40), calls=%async_computation | async-start | bytes 32768 | tf_op jit(solution)/shard_map/all_to_all | solution.py:273
  28.7 6.4 %grads.1 = (bf16[4096,1024]{1,0:T(8,128)(2,1)}, bf16[1024,4096]{1,0:T(8,128)(2,1)}, bf16[32,4096]{1,0:T(8,128)(2,1)S(1)}) custom-call(bf16[32,4096]{1,0:T(8,128)(2,1)S(1)} %get-tuple-element.33.x, bf16[32,4096]{1,0:T(8,128)(2,1)S(1)} %get-tuple-element.34.gs, bf16[32,1024]{1,0:T(8,128)(2,1)S(1)} %get-tuple-element.35.hidden, ...), custom_call_target="tpu_custom_call" | custom-call | tf_op jit(solution)/shard_map/grads/pallas_call | solution.py:212
  35.2 0.6 %all-to-all-done.terms = f32[32,1,32]{2,1,0:T(1,128)S(1)} async-done(((f32[32,1,32]{2,1,0:T(1,128)}), f32[32,1,32]{2,1,0:T(1,128)S(1)}, u32[]{:S(2)}, u32[]{:S(2)}) %all-to-all-start) | async-done | bytes 4128 | tf_op jit(solution)/shard_map/all_to_all | solution.py:273
  35.8 0.8 %router.1 = f32[4,4096]{1,0:T(4,128)} custom-call(s32[2,32]{1,0:T(2,128)S(1)} %get-tuple-element.28.ids, bf16[32,4096]{1,0:T(8,128)(2,1)S(1)} %get-tuple-element.39.x, f32[32,1,32]{2,1,0:T(1,128)S(1)} %all-to-all-done.terms), custom_call_target="tpu_custom_call" | custom-call | tf_op jit(solution)/shard_map/router/pallas_call | solution.py:246
Async XLA Ops:
  1.4 9.2 %collective-permute-start = (bf16[1,2,4096]{2,1,0:T(2,128)(2,1)S(1)}, bf16[1,2,4096]{2,1,0:T(2,128)(2,1)S(1)}, u32[]{:S(2)}, u32[]{:S(2)}) collective-permute-start(bf16[1,2,4096]{2,1,0:T(2,128)(2,1)S(1)} %pack.1), channel_id=1, source_target_pairs={{0,24},{1,25},{2,26},{3,27},{4,28},{5,29},{6,30},{7,31},{8,16},{9,... | collective-permute-start | bytes 49160 | tf_op jit(solution)/shard_map/ppermute | solution.py:64
  6.5 4.6 %collective-permute-start.1 = (bf16[1,2,4096]{2,1,0:T(2,128)(2,1)S(1)}, bf16[1,2,4096]{2,1,0:T(2,128)(2,1)S(1)}, u32[]{:S(2)}, u32[]{:S(2)}) collective-permute-start(bf16[1,2,4096]{2,1,0:T(2,128)(2,1)S(1)} %pack.1), channel_id=1, source_target_pairs={{0,16},{1,17},{2,18},{3,19},{4,20},{5,21},{6,22},{7,23},{8,24},{9,... | collective-permute-start | bytes 49160 | tf_op jit(solution)/shard_map/ppermute | solution.py:64
  6.5 4.6 %collective-permute-start.2 = (bf16[1,2,4096]{2,1,0:T(2,128)(2,1)S(1)}, bf16[1,2,4096]{2,1,0:T(2,128)(2,1)S(1)}, u32[]{:S(2)}, u32[]{:S(2)}) collective-permute-start(bf16[1,2,4096]{2,1,0:T(2,128)(2,1)S(1)} %pack.1), channel_id=1, source_target_pairs={{0,8},{1,9},{2,10},{3,11},{4,12},{5,13},{6,14},{7,15},{8,0},{9,1},... | collective-permute-start | bytes 49160 | tf_op jit(solution)/shard_map/ppermute | solution.py:64
  11.3 6.4 %collective-permute-start.3 = (bf16[4,2,4096]{2,1,0:T(2,128)(2,1)S(1)}, bf16[4,2,4096]{2,1,0:T(2,128)(2,1)S(1)}, u32[]{:S(2)}, u32[]{:S(2)}) collective-permute-start(bf16[4,2,4096]{2,1,0:T(2,128)(2,1)S(1)} %pad_maximum_fusion.1), channel_id=1, source_target_pairs={{0,6},{1,7},{2,4},{3,5},{4,2},{5,3},{6,0},{7,1},{8,14},{9,15},{10,... | collective-permute-start | bytes 196616 | tf_op jit(solution)/shard_map/ppermute | solution.py:64
  13.8 4.3 %collective-permute-start.4 = (bf16[4,2,4096]{2,1,0:T(2,128)(2,1)S(1)}, bf16[4,2,4096]{2,1,0:T(2,128)(2,1)S(1)}, u32[]{:S(2)}, u32[]{:S(2)}) collective-permute-start(bf16[4,2,4096]{2,1,0:T(2,128)(2,1)S(1)} %pad_maximum_fusion.1), channel_id=1, source_target_pairs={{0,4},{1,5},{2,6},{3,7},{4,0},{5,1},{6,2},{7,3},{8,12},{9,13},{10,... | collective-permute-start | bytes 196616 | tf_op jit(solution)/shard_map/ppermute | solution.py:64
  14.3 4.3 %collective-permute-start.5 = (bf16[4,2,4096]{2,1,0:T(2,128)(2,1)S(1)}, bf16[4,2,4096]{2,1,0:T(2,128)(2,1)S(1)}, u32[]{:S(2)}, u32[]{:S(2)}) collective-permute-start(bf16[4,2,4096]{2,1,0:T(2,128)(2,1)S(1)} %pad_maximum_fusion.1), channel_id=1, source_target_pairs={{0,2},{1,3},{2,0},{3,1},{4,6},{5,7},{6,4},{7,5},{8,10},{9,11},{10,... | collective-permute-start | bytes 196616 | tf_op jit(solution)/shard_map/ppermute | solution.py:64
  19.0 1.7 %collective-permute-start.6 = (bf16[16,2,4096]{2,1,0:T(2,128)(2,1)S(1)}, bf16[16,2,4096]{2,1,0:T(2,128)(2,1)S(1)}, u32[]{:S(2)}, u32[]{:S(2)}) collective-permute-start(bf16[16,2,4096]{2,1,0:T(2,128)(2,1)S(1)} %pad_maximum_fusion.mine), channel_id=1, source_target_pairs={{0,1},{1,0},{2,3},{3,2},{4,5},{5,4},{6,7},{7,6},{8,9},{9,8},{10,11... | collective-permute-start | bytes 786440 | tf_op jit(solution)/shard_map/ppermute | solution.py:269
  24.1 11.7 %all-to-all-start = ((f32[32,1,32]{2,1,0:T(1,128)}), f32[32,1,32]{2,1,0:T(1,128)S(1)}, u32[]{:S(2)}, u32[]{:S(2)}) async-start(f32[32,1,32]{2,1,0:T(1,128)} %get-tuple-element.40), calls=%async_computation | async-start | bytes 32768 | tf_op jit(solution)/shard_map/all_to_all | solution.py:273
